TPU v7x, 128 devices: a whole 4x4x4 slice. The times are simulated.
128 devices in a mesh: row: 16 (over y, x_lo, core), list: 8 (over z, x_hi).
Axes of the slice: x: 4 (x_hi: 2, x_lo: 2; x = x_hi * 2 + x_lo), y: 4, z: 4, core: 2. Of those that a mesh axis runs over, the one named last changes fastest.
Arguments:
- key_rows: bfloat16 [16384, 256], P('row'), may hold values from -88 to 88
- centroids: bfloat16 [49152, 256], P('list'), may hold values from -32 to 32
Outputs:
- new_centroids: bfloat16 [49152, 256], P('list')
- row_potential: float32 [16384], P('row')
- list_potential: float32 [49152], P('list')
All inputs are finite; a program needn't handle non-finite values.
Results may differ from a plain program's by a relative error of at most 0.0047.
Values may be sent and summed in bfloat16 or wider, within the bound.
A program may use at most 64 MiB of HBM per device.

v0:
```python
import math

import jax
import jax.numpy as jnp
from jax import lax
from jax.sharding import PartitionSpec as P

ITERS = 2


def scored_tile(key_rows, cent_tile):
    factor = 2.0 / math.sqrt(key_rows.shape[1])
    return (
        lax.dot_general(
            key_rows, cent_tile, (((1,), (1,)), ((), ())), preferred_element_type=jnp.float32
        )
        * factor
    )


def row_update(key_rows, centroids, list_potential, n_keys):
    n_local = centroids.shape[0]
    span = math.gcd(n_local, 1024)
    tiles = centroids.reshape(n_local // span, span, centroids.shape[1])
    pots = list_potential.reshape(n_local // span, span)
    count_rows = key_rows.shape[0]

    def advance(carry, item):
        peak, total = carry
        scored = scored_tile(key_rows, item[0]) + item[1][None, :]
        top = jnp.maximum(peak, jnp.max(scored, axis=1))
        total = total * jnp.exp(peak - top) + jnp.sum(jnp.exp(scored - top[:, None]), axis=1)
        return ((top, total), None)

    start = (jnp.full((count_rows,), -1e30, jnp.float32), jnp.zeros((count_rows,), jnp.float32))
    (peak, total), unused = lax.scan(advance, start, (tiles, pots))
    highest = lax.pmax(peak, "list")
    total = lax.psum(total * jnp.exp(peak - highest), "list")
    peak = highest
    return -math.log(n_keys) - (peak + jnp.log(total))


def col_update(key_rows, centroids, row_potential, n_lists):
    n_local = centroids.shape[0]
    span = math.gcd(n_local, 1024)
    tiles = centroids.reshape(n_local // span, span, centroids.shape[1])

    def column_stats(tile):
        scored = scored_tile(key_rows, tile) + row_potential[:, None]
        top = jnp.max(scored, axis=0)
        return (top, jnp.sum(jnp.exp(scored - top[None, :]), axis=0))

    peak, total = lax.map(column_stats, tiles)
    peak = peak.reshape(n_local)
    total = total.reshape(n_local)
    highest = lax.pmax(peak, "row")
    total = lax.psum(total * jnp.exp(peak - highest), "row")
    peak = highest
    return -math.log(n_lists) - (peak + jnp.log(total))


def local(key_rows, centroids):
    n_keys = key_rows.shape[0] * lax.axis_size("row")
    n_local = centroids.shape[0]
    n_lists = n_local * lax.axis_size("list")
    list_potential = jnp.zeros((n_local,), jnp.float32)
    row_potential = jnp.zeros((key_rows.shape[0],), jnp.float32)
    for sweep in range(ITERS):
        row_potential = row_update(key_rows, centroids, list_potential, n_keys)
        list_potential = col_update(key_rows, centroids, row_potential, n_lists)
    scored = scored_tile(key_rows, centroids)
    weights = jnp.exp(
        scored + row_potential[:, None] + list_potential[None, :] + math.log(n_lists)
    ).astype(jnp.bfloat16)
    summed = lax.psum(
        lax.dot_general(
            weights, key_rows, (((0,), (0,)), ((), ())), preferred_element_type=jnp.float32
        ),
        "row",
    )
    new_centroids = summed.astype(jnp.bfloat16)
    return (new_centroids, row_potential, list_potential)


def solution(mesh):
    return jax.shard_map(
        local,
        mesh=mesh,
        in_specs=(P("row", None), P("list", None)),
        out_specs=(P("list", None), P("row"), P("list")),
        check_vma=False,
    )
```

profile of v0, /device:TPU:1, one launch (start us, length us, event | category | flops | bytes accessed | tf_op | source)
XLA Modules:
  0.0 516.7 jit_solution(3106630791439869775)
XLA Ops:
  0.7 16.5 %while.52 = (s32[]{:T(128)}, f32[1024]{0:T(1024)S(1)}, f32[1024]{0:T(1024)S(1)}, bf16[6,1024,256]{2,1,0:T(8,128)(2,1)}, bf16[1024,256]{1,0:T(8,128)(2,1)}, /*index=5*/s32[]{:T(128)}, s32[]{:T(128)}) while((s32[]{:T(128)}, f32[1024]{0:T(1024)S(1)}, f32[1024]{0:T(1024)S(1)}, bf16[6,1024,256]{2,1,0:T(8,128)(2,1)}, ...), condition=%wide.region_3.4_spmd.clone, body=%wide.region_0.3_spmd.clone.sunk | while | flops 542118912 | bytes 9490532 | solution.py:36
  17.1 22.6 %pmax.28 = f32[1024]{0:T(1024)S(1)} all-reduce(f32[1024]{0:T(1024)S(1)} %get-tuple-element.130), channel_id=1, replica_groups=mesh['row'=16,'list'=8] {'list'}, use_global_device_ids=true, to_apply=%region_4.5 | all-reduce | flops 1024 | bytes 8192 | tf_op jit(solution)/shard_map/pmax | solution.py:37
  39.8 15.6 %psum.35 = f32[1024]{0:T(1024)S(1)} all-reduce(f32[1024]{0:T(1024)S(1)} %exponential_multiply_fusion.3), channel_id=1, replica_groups=mesh['row'=16,'list'=8] {'list'}, use_global_device_ids=true, to_apply=%region_5.6 | all-reduce | flops 1024 | bytes 8192 | tf_op jit(solution)/shard_map/psum | solution.py:38
  55.4 18.6 %while.50 = (s32[]{:T(128)}, f32[6,1024]{1,0:T(8,128)S(1)}, f32[6,1024]{1,0:T(8,128)S(1)}, bf16[6,1024,256]{2,1,0:T(8,128)(2,1)}, bf16[1024,256]{1,0:T(8,128)(2,1)}, /*index=5*/f32[1024]{0:T(1024)S(1)}, s32[]{:T(128)}, s32[]{:T(128)}) while((s32[]{:T(128)}, f32[6,1024]{1,0:T(8,128)S(1)}, f32[6,1024]{1,0:T(8,128)S(1)}, ...), condition=%wide.region_9.10_spmd, body=%wide.region_6.9_spmd.sunk | while | flops 544208896 | bytes 9474153 | solution.py:53
  55.4 2.0 fusion.43
  58.5 2.0 fusion.43
  61.6 2.0 fusion.43
  67.8 2.0 fusion.43
  70.9 2.0 fusion.43
  74.0 56.4 %pmax.29 = f32[6144]{0:T(1024)S(1)} all-reduce(f32[6144]{0:T(1024)S(1)} %reshape.36), channel_id=1, replica_groups=mesh['row'=16,'list'=8] {'row'}, use_global_device_ids=true, to_apply=%region_10.11 | all-reduce | flops 6144 | bytes 49152 | tf_op jit(solution)/shard_map/pmax | solution.py:56
  130.5 52.9 %psum.36 = f32[6144]{0:T(1024)S(1)} all-reduce(f32[6144]{0:T(1024)S(1)} %exponential_multiply_fusion.1), channel_id=1, replica_groups=mesh['row'=16,'list'=8] {'row'}, use_global_device_ids=true, to_apply=%region_11.12 | all-reduce | flops 6144 | bytes 49152 | tf_op jit(solution)/shard_map/psum | solution.py:57
  183.4 17.6 %while.53 = (s32[]{:T(128)}, f32[1024]{0:T(1024)S(1)}, f32[1024]{0:T(1024)S(1)}, bf16[6,1024,256]{2,1,0:T(8,128)(2,1)}, bf16[1024,256]{1,0:T(8,128)(2,1)}, /*index=5*/f32[6,1024]{1,0:T(8,128)S(1)}, s32[]{:T(128)}, s32[]{:T(128)}) while((s32[]{:T(128)}, f32[1024]{0:T(1024)S(1)}, f32[1024]{0:T(1024)S(1)}, ...), condition=%wide.region_15.16_spmd.clone, body=%wide.region_12.15_spmd.clone.sunk | while | flops 544216064 | bytes 9506928 | solution.py:36
  186.4 2.0 fusion.49
  192.3 2.0 fusion.49
  198.1 2.0 fusion.49
  201.0 18.8 %pmax.30 = f32[1024]{0:T(1024)S(1)} all-reduce(f32[1024]{0:T(1024)S(1)} %get-tuple-element.134), channel_id=1, replica_groups=mesh['row'=16,'list'=8] {'list'}, use_global_device_ids=true, to_apply=%region_16.17 | all-reduce | flops 1024 | bytes 8192 | tf_op jit(solution)/shard_map/pmax | solution.py:37
  219.9 15.6 %psum.37 = f32[1024]{0:T(1024)S(1)} all-reduce(f32[1024]{0:T(1024)S(1)} %exponential_multiply_fusion.2), channel_id=1, replica_groups=mesh['row'=16,'list'=8] {'list'}, use_global_device_ids=true, to_apply=%region_17.18 | all-reduce | flops 1024 | bytes 8192 | tf_op jit(solution)/shard_map/psum | solution.py:38
  235.5 18.6 %while.51 = (s32[]{:T(128)}, f32[6,1024]{1,0:T(8,128)S(1)}, f32[6,1024]{1,0:T(8,128)S(1)}, bf16[6,1024,256]{2,1,0:T(8,128)(2,1)}, bf16[1024,256]{1,0:T(8,128)(2,1)}, /*index=5*/f32[1024]{0:T(1024)S(1)}, s32[]{:T(128)}, s32[]{:T(128)}) while((s32[]{:T(128)}, f32[6,1024]{1,0:T(8,128)S(1)}, f32[6,1024]{1,0:T(8,128)S(1)}, ...), condition=%wide.region_21.22_spmd, body=%wide.region_18.21_spmd.sunk | while | flops 544208896 | bytes 9474153 | solution.py:53
  238.6 2.0 fusion.45
  247.9 2.0 fusion.45
  254.2 60.2 %pmax.31 = f32[6144]{0:T(1024)S(1)} all-reduce(f32[6144]{0:T(1024)S(1)} %reshape.39), channel_id=1, replica_groups=mesh['row'=16,'list'=8] {'row'}, use_global_device_ids=true, to_apply=%region_22.23 | all-reduce | flops 6144 | bytes 49152 | tf_op jit(solution)/shard_map/pmax | solution.py:56
  314.3 53.1 %psum.38 = f32[6144]{0:T(1024)S(1)} all-reduce(f32[6144]{0:T(1024)S(1)} %exponential_multiply_fusion), channel_id=1, replica_groups=mesh['row'=16,'list'=8] {'row'}, use_global_device_ids=true, to_apply=%region_23.24 | all-reduce | flops 6144 | bytes 49152 | tf_op jit(solution)/shard_map/psum | solution.py:57
  367.4 12.8 %fusion.21 = f32[6144,256]{1,0:T(8,128)} fusion(bf16[1024,256]{1,0:T(8,128)(2,1)} %get-tuple-element.485, f32[6144]{0:T(1024)S(1)} %add_subtract_fusion, f32[1024]{0:T(1024)S(1)} %get-tuple-element.490, bf16[6144,256]{1,0:T(8,128)(2,1)} %bitcast.60), kind=kOutput, calls=%fused_computation.35 | convolution fusion | flops 6473908224 | bytes 9990144 | tf_op jit(solution)/shard_map/dot_general | solution.py:76
  380.2 136.5 %all-reduce.1 = bf16[6144,256]{1,0:T(8,128)(2,1)} all-reduce(f32[6144,256]{1,0:T(8,128)} %fusion.21), channel_id=1, replica_groups=mesh['row'=16,'list'=8] {'row'}, use_global_device_ids=true, to_apply=%region_24.25 | all-reduce | flops 1572864 | bytes 9437184 | tf_op jit(solution)/shard_map/psum | solution.py:75
  (129 shorter events, 50.7 us)
Async XLA Ops:
  254.1 126.1 %copy-start = (f32[1024]{0:T(1024)}, f32[1024]{0:T(1024)S(1)}, u32[]{:S(2)}) copy-start(f32[1024]{0:T(1024)S(1)} %get-tuple-element.490) | copy-start | bytes 12292
  367.4 12.8 %copy-start.1 = (f32[6144]{0:T(1024)}, f32[6144]{0:T(1024)S(1)}, u32[]{:S(2)}) copy-start(f32[6144]{0:T(1024)S(1)} %add_subtract_fusion) | copy-start | bytes 73732
where the time goes:
time: 521 us; the launch traced here: 517 us
  blocking collectives  432 us (83%)
  matrix products  59.7 us (11%)
  other arithmetic  20.6 us (4%)
    psum x1, blocking collectives, local(): lax.psum(lax.dot_general(weights, key_rows, (((0,), (0,)), ((), ())), pre...  136 us
    pmax x2, blocking collectives, col_update(): highest = lax.pmax(peak, 'row')  117 us
    psum x2, blocking collectives, col_update(): total = lax.psum(total * jnp.exp(peak - highest), 'row')  106 us
    dot_general x24, matrix products, scored_tile(): lax.dot_general(key_rows, cent_tile, (((1,), (1,)), ((), ())), preferred_...  47 us
    pmax x2, blocking collectives, row_update(): highest = lax.pmax(peak, 'list')  41.4 us
    psum x2, blocking collectives, row_update(): total = lax.psum(total * jnp.exp(peak - highest), 'list')  31.2 us
    dot_general x1, matrix products, local(): lax.dot_general(weights, key_rows, (((0,), (0,)), ((), ())), preferred_el...  12.8 us
    reduce_sum x12, other arithmetic, column_stats(): return (top, jnp.sum(jnp.exp(scored - top[None, :]), axis=0))  10.6 us

commit v1 on v0

v1 whole, which is shorter than its diff:
```python
import math

import jax
import jax.numpy as jnp
from jax import lax
from jax.experimental import pallas as pl
from jax.experimental.pallas import tpu as pltpu
from jax.sharding import PartitionSpec as P

MESH = pl.DeviceIdType.MESH
f32 = jnp.float32
bf16 = jnp.bfloat16
LOG2E = math.log2(math.e)
LN2 = math.log(2.0)

D = 256
SCALE = 2.0 / math.sqrt(D) * LOG2E
NK = 1024
NL = 6144
W = 512
NT = NL // W
N_ROW, N_LIST, CHIPS, CORES = 16, 8, 8, 2
SHARE = NL // CHIPS
BLOCKS = SHARE // 128
LB = 256
NCH = SHARE // LB
KT = 1024
STEPS = CHIPS * NK // (2 * KT)
LOG2_KEYS = math.log2(NK * N_ROW)
LOG2_LISTS = math.log2(NL * N_LIST)
NT_DIMS = (((1,), (1,)), ((), ()))
NN_DIMS = (((1,), (0,)), ((), ()))


def tree(op, xs):
    xs = list(xs)
    while len(xs) > 1:
        ys = [op(a, b) for a, b in zip(xs[::2], xs[1::2])]
        if len(xs) % 2:
            ys.append(xs[-1])
        xs = ys
    return xs[0]


def log2(x):
    return jnp.log(x) * LOG2E


def fold(op, x):
    return tree(op, [x[8 * i : 8 * i + 8] for i in range(x.shape[0] // 8)])


def row_pass(keys, cents, scores, peak, total):
    peak[...] = jnp.full(peak.shape, -1e30, f32)
    total[...] = jnp.zeros(total.shape, f32)
    rb = 32

    def body(i, carry):
        for half in range(2):
            t = 2 * i + half
            lists = pl.ds(pl.multiple_of(t * W, W), W)
            s = lax.dot_general(keys[...], cents[lists, :], NT_DIMS, preferred_element_type=f32) * SCALE
            scores[t] = s
            for b in range(NK // rb):
                rows = slice(b * rb, (b + 1) * rb)
                xs = [s[rows, v * 128 : (v + 1) * 128] for v in range(W // 128)]
                before = peak[rows, :]
                top = jnp.maximum(before, tree(jnp.maximum, xs))
                sums = tree(jnp.add, [jnp.exp2(x - top) for x in xs])
                total[rows, :] = total[rows, :] * jnp.exp2(before - top) + sums
                peak[rows, :] = top
        return carry

    lax.fori_loop(0, NT // 2, body, 0)


def column_pass(scores, row_pot, stats, first, last):
    rb = 256

    def body(i, carry):
        for v in range(W // 128):
            lanes = slice(v * 128, (v + 1) * 128)
            tops = []
            for b in range(NK // rb):
                rows = slice(b * rb, (b + 1) * rb)
                x = scores[i, rows, lanes] + row_pot[rows, :]
                scores[i, rows, lanes] = x
                tops.append(fold(jnp.maximum, x))
            top = jnp.max(tree(jnp.maximum, tops), axis=0, keepdims=True)
            sums = []
            for b in range(NK // rb):
                rows = slice(b * rb, (b + 1) * rb)
                e = jnp.exp2(scores[i, rows, lanes] - top)
                scores[i, rows, lanes] = e
                sums.append(fold(jnp.add, e))
            total = jnp.sum(tree(jnp.add, sums), axis=0, keepdims=True)
            j = i * (W // 128) + v
            q, at = lax.div(j, BLOCKS), lax.rem(j, BLOCKS)
            stats[pl.ds(q, 1), 0, pl.ds(at, 1), :] = top[None]
            stats[pl.ds(q, 1), 1, pl.ds(at, 1), :] = total[None]
        return carry

    lax.fori_loop(first, last, body, 0)


def row_sums(scores, gain, total):
    rb, group = 64, 4

    def body(i, carry):
        def at(b):
            return pl.ds(pl.multiple_of(i * rb + 8 * b, 8), 8)

        def inner(c, accs):
            accs = list(accs)
            for t in range(group):
                for v in range(W // 128):
                    lanes = slice(v * 128, (v + 1) * 128)
                    g = gain[c * group + t, :, lanes]
                    for b in range(rb // 8):
                        accs[b] = accs[b] + scores[c * group + t, at(b), lanes] * g
            return tuple(accs)

        zero = jnp.zeros((8, 128), f32)
        accs = lax.fori_loop(0, NT // group, inner, (zero,) * (rb // 8))
        for b in range(rb // 8):
            total[at(b), :] = accs[b]
        return carry

    lax.fori_loop(0, NK // rb, body, 0)


def column_sums(scores, factor, sums):
    rb = 128

    def body(i, carry):
        accs = [[] for _ in range(W // 128)]
        for b in range(NK // rb):
            rows = slice(b * rb, (b + 1) * rb)
            u = factor[rows, :]
            for v in range(W // 128):
                part = fold(jnp.add, scores[i, rows, v * 128 : (v + 1) * 128] * u)
                accs[v] = part if b == 0 else accs[v] + part
        for v in range(W // 128):
            j = i * (W // 128) + v
            q, at = lax.div(j, BLOCKS), lax.rem(j, BLOCKS)
            sums[pl.ds(q, 1), pl.ds(at, 1), :] = jnp.sum(accs[v], axis=0, keepdims=True)[None]
        return carry

    lax.fori_loop(0, NT, body, 0)


def spread(compact, n, out):
    for b in range(n):
        out[b * 128 : (b + 1) * 128, :] = jnp.broadcast_to(compact[b : b + 1, :], (128, 128)).T


def remote(src, dst, send, recv, target):
    return pltpu.make_async_remote_copy(
        src_ref=src, dst_ref=dst, send_sem=send, recv_sem=recv, device_id=target, device_id_type=MESH
    )


class Gather:
    def __init__(self, at, send, recv, y, x, core, twin=False, own=None):
        self.at, self.send, self.recv, self.twin = at, send, recv, twin
        self.core = core
        self.own = own

        def chip(dy, flip):
            return lax.rem(y + dy + 4, 4) * 2 + (1 - x if flip else x)

        self.chip = chip
        self.up = {"row": chip(1, False) * 2 + core}
        self.down = {"row": chip(-1, False) * 2 + core}
        self.side = {"row": chip(0, True) * 2 + core}
        self.other = {"row": chip(0, False) * 2 + 1 - core}
        self.moves = [
            (self.up, (0, False), (-1, False), None),
            (self.down, (0, False), (1, False), None),
            (self.side, (0, False), (0, True), None),
            (self.up, (-1, False), (-2, False), 0),
            (self.down, (1, False), (2, False), 1),
            (self.up, (0, True), (-1, True), None),
            (self.down, (0, True), (1, True), None),
            (self.side, (-2, False), (2, True), 0),
            (self.side, (2, False), (2, True), 1),
        ]

    def source(self, block, part):
        if self.own is not None and block == (0, False):
            return self.own
        return self.at(self.chip(*block), part)

    def copy(self, m):
        target, sent, _, part = self.moves[m]
        place = self.at(self.chip(*sent), part)
        return remote(self.source(sent, part), place, self.send.at[m], self.recv.at[m], target)

    def arrival(self, m):
        target, _, came, part = self.moves[m]
        place = self.at(self.chip(*came), part)
        return remote(place, place, self.send.at[m], self.recv.at[m], target)

    def hand(self, m):
        block, part = ((0, False), None) if m == 9 else self.moves[m][2:]
        place = self.at(self.chip(*block), part)
        return remote(self.source(block, part), place, self.send.at[10 + m], self.recv.at[10 + m], self.other)

    def handed(self, m):
        block, part = ((0, False), None) if m == 9 else self.moves[m][2:]
        place = self.at(self.chip(*block), part, 1 - self.core)
        return remote(place, place, self.send.at[10 + m], self.recv.at[10 + m], self.other)

    def take(self, arrivals, sends):
        for m in arrivals:
            self.arrival(m).wait_recv()
            for s in sends.get(m, ()):
                self.copy(s).start()
            if self.twin:
                self.hand(m).start()

    def stage1(self):
        for m in (0, 1, 2):
            self.copy(m).start()
        if self.twin:
            self.hand(9).start()

    def stage2(self):
        self.take((0, 1, 2), {0: (3,), 1: (4,), 2: (5, 6)})

    def stage3(self):
        self.take((3, 4), {3: (7,), 4: (8,)})

    def stage4(self):
        self.take((5, 6, 7, 8), {})

    def finish(self):
        for m in range(9):
            self.copy(m).wait_send()
        if self.twin:
            for m in range(10):
                self.hand(m).wait_send()
                self.handed(m).wait_recv()


def kernel(
    keys, cents, new_ref, rowpot_ref, listpot_ref,
    scores, peak, total, row_pot, gain, stats, sums, pots, pots2, from_list1, from_list3, from_row2, from_row4,
    row_all, keys_all, row_lanes, list_lanes, sa, sb, acc, came, done,
    list1_s, list1_r, list3_s, list3_r, row2_s, row2_r, row4_s, row4_r, pot_s, pot_r, pot2_s, pot2_r, all_s, all_r,
    keys_s, keys_r, twin_s, twin_r, out_s, out_r, here,
):
    row, lst = lax.axis_index("row"), lax.axis_index("list")
    core, chip = lax.rem(row, 2), lax.div(row, 2)
    x, y = lax.rem(chip, 2), lax.div(chip, 2)

    barrier = pltpu.get_barrier_semaphore()
    for k in range(1, N_ROW):
        pl.semaphore_signal(barrier, inc=1, device_id={"row": lax.rem(row + k, N_ROW)}, device_id_type=MESH)
    for k in range(1, N_LIST):
        pl.semaphore_signal(barrier, inc=1, device_id={"list": lax.rem(lst + k, N_LIST)}, device_id_type=MESH)
    stats[...] = jnp.zeros(stats.shape, f32)
    sums[...] = jnp.zeros(sums.shape, f32)
    keys_all[chip] = keys[...]
    pl.semaphore_wait(barrier, N_ROW + N_LIST - 2)

    def keys_at(q, part):
        return keys_all.at[q] if part is None else keys_all.at[q, pl.ds(part * (NK // 2), NK // 2)]

    gather = Gather(keys_at, keys_s, keys_r, y, x, core)
    gather.stage1()

    def to_list(buf, send, recv):
        for k in range(1, N_LIST):
            remote(buf.at[lst], buf.at[lst], send.at[k], recv.at[lst], {"list": lax.rem(lst + k, N_LIST)}).start()

    def from_list(buf, send, recv):
        for k in range(1, N_LIST):
            src = lax.rem(lst + k, N_LIST)
            remote(buf.at[src], buf.at[src], send.at[k], recv.at[src], {"list": src}).wait_recv()
        for k in range(1, N_LIST):
            remote(buf.at[lst], buf.at[lst], send.at[k], recv.at[lst], {"list": lax.rem(lst + k, N_LIST)}).wait_send()

    def to_row(src_of, buf, send, recv):
        for k in range(1, N_ROW):
            to = lax.rem(row + k, N_ROW)
            remote(src_of.at[lax.div(to, 2)], buf.at[row], send.at[k], recv.at[row], {"row": to}).start()

    def from_row(src_of, buf, send, recv):
        for k in range(1, N_ROW):
            src = lax.rem(row + k, N_ROW)
            remote(buf.at[src], buf.at[src], send.at[k], recv.at[src], {"row": src}).wait_recv()
        for k in range(1, N_ROW):
            to = lax.rem(row + k, N_ROW)
            remote(src_of.at[lax.div(to, 2)], buf.at[row], send.at[k], recv.at[row], {"row": to}).wait_send()

    def to_chips(buf, send, recv):
        for k in range(1, CHIPS):
            to = lax.rem(chip + k, CHIPS) * 2 + core
            remote(buf.at[chip], buf.at[chip], send.at[k], recv.at[chip], {"row": to}).start()

    def from_chips(buf, send, recv):
        for k in range(1, CHIPS):
            src = lax.rem(chip + k, CHIPS)
            remote(buf.at[src], buf.at[src], send.at[k], recv.at[src], {"row": src * 2 + core}).wait_recv()
        for k in range(1, CHIPS):
            to = lax.rem(chip + k, CHIPS) * 2 + core
            remote(buf.at[chip], buf.at[chip], send.at[k], recv.at[chip], {"row": to}).wait_send()

    row_pass(keys, cents, scores, peak, total)
    for b in range(NK // 128):
        rows = slice(b * 128, (b + 1) * 128)
        top = peak[rows, :].T
        best = jnp.max(top, axis=0, keepdims=True)
        part = jnp.sum(total[rows, :].T * jnp.exp2(top - best), axis=0, keepdims=True)
        from_list1[lst, 0, b : b + 1, :] = best
        from_list1[lst, 1, b : b + 1, :] = part
    to_list(from_list1, list1_s, list1_r)
    from_list(from_list1, list1_s, list1_r)
    best = tree(jnp.maximum, [from_list1[k, 0] for k in range(N_LIST)])
    whole = tree(jnp.add, [from_list1[k, 1] * jnp.exp2(from_list1[k, 0] - best) for k in range(N_LIST)])
    row1 = -LOG2_KEYS - (best + log2(whole))
    spread(row1, NK // 128, row_pot)

    column_pass(scores, row_pot, stats, 0, 4)
    gather.stage2()
    column_pass(scores, row_pot, stats, 4, NT)
    from_row2[row] = stats[chip]
    to_row(stats, from_row2, row2_s, row2_r)
    from_row(stats, from_row2, row2_s, row2_r)
    best = tree(jnp.maximum, [from_row2[k, 0] for k in range(N_ROW)])
    whole = tree(jnp.add, [from_row2[k, 1] * jnp.exp2(from_row2[k, 0] - best) for k in range(N_ROW)])
    pots[chip] = -LOG2_LISTS - (best + log2(whole))
    to_chips(pots, pot_s, pot_r)
    gather.stage3()
    from_chips(pots, pot_s, pot_r)

    for q in range(CHIPS):
        g = jnp.exp2(stats[q, 0] + pots[q])
        stats[q, 1] = g
        for b in range(BLOCKS):
            j = q * BLOCKS + b
            v = j % (W // 128)
            gain[j // (W // 128), :, v * 128 : (v + 1) * 128] = jnp.broadcast_to(g[b : b + 1, :], (8, 128))
    row_sums(scores, gain, total)
    for b in range(NK // 128):
        from_list3[lst, b : b + 1, :] = jnp.sum(total[b * 128 : (b + 1) * 128, :].T, axis=0, keepdims=True)
    to_list(from_list3, list3_s, list3_r)
    from_list(from_list3, list3_s, list3_r)
    delta = -LOG2_KEYS - log2(tree(jnp.add, [from_list3[k] for k in range(N_LIST)]))
    row2 = row1 + delta
    row_all[chip] = row2
    to_chips(row_all, all_s, all_r)
    rowpot_ref[...] = row2 * LN2
    spread(jnp.exp2(delta), NK // 128, row_pot)

    column_sums(scores, row_pot, sums)
    for q in range(CHIPS):
        sums[q] = sums[q] * stats[q, 1]
    from_row4[row] = sums[chip]
    to_row(sums, from_row4, row4_s, row4_r)
    gather.stage4()
    from_chips(row_all, all_s, all_r)
    for q in range(CHIPS):
        for b in range(NK // 128):
            row_lanes[:, (q * 8 + b) * 128 : (q * 8 + b + 1) * 128] = row_all[q, b : b + 1, :]
    from_row(sums, from_row4, row4_s, row4_r)
    list2 = pots[chip] - LOG2_LISTS - log2(tree(jnp.add, [from_row4[k] for k in range(N_ROW)]))
    pots2[chip] = list2
    to_chips(pots2, pot2_s, pot2_r)
    spread(list2 + LOG2_LISTS, BLOCKS, list_lanes)
    gather.finish()

    def chunk_at(ch):
        def at(q, part, of=core):
            base = q * SHARE + ch * LB + of * (LB // 2)
            if part is None:
                return new_ref.at[pl.ds(pl.multiple_of(base, LB // 2), LB // 2)]
            return new_ref.at[pl.ds(pl.multiple_of(base + part * (LB // 4), LB // 4), LB // 4)]

        return at

    outs = [
        Gather(chunk_at(ch), out_s.at[ch], out_r.at[ch], y, x, core, twin=True, own=done.at[ch]) for ch in range(NCH)
    ]
    twin = {"row": chip * 2 + 1 - core}
    mine = pl.multiple_of(core * (LB // 2), LB // 2)
    theirs = pl.multiple_of((1 - core) * (LB // 2), LB // 2)

    def swap(ch):
        return remote(acc.at[ch, pl.ds(theirs, LB // 2)], came.at[ch], twin_s.at[ch], twin_r.at[ch], twin)

    def keep(ch):
        return pltpu.make_async_copy(done.at[ch], chunk_at(ch)(chip, None), here.at[ch])

    def begin(ch):
        swap(ch).wait()
        done[ch] = (acc[ch, pl.ds(mine, LB // 2), :] + came[ch]).astype(bf16)
        outs[ch].stage1()
        keep(ch).start()

    def tile(t):
        return keys_all[lax.div(t * KT, NK)]

    def mm1(ch, t):
        c = cents[pl.ds(pl.multiple_of(chip * SHARE + ch * LB, LB), LB), :]
        return lax.dot_general(c, tile(t), NT_DIMS, preferred_element_type=f32)

    def weigh(s_ref, ch, t):
        c = list_lanes[pl.ds(pl.multiple_of(ch * LB, LB), LB), :]
        out = []
        for v in range(KT // 128):
            r = row_lanes[:, pl.ds(pl.multiple_of(t * KT + v * 128, 128), 128)]
            s = s_ref[:, v * 128 : (v + 1) * 128] * SCALE
            out.append(jnp.exp2((s + r) + c).astype(bf16))
        return jnp.concatenate(out, axis=1)

    def mm2(w, t):
        return lax.dot_general(w, tile(t), NN_DIMS, preferred_element_type=f32)

    acc[...] = jnp.zeros(acc.shape, f32)
    sa[...] = mm1(0, 0)

    def step(i, carry):
        ch, t = lax.div(i, STEPS), 2 * lax.rem(i, STEPS)
        nxt = lax.rem(i + 1, NCH * STEPS)
        sb[...] = mm1(ch, t + 1)
        first = mm2(weigh(sa, ch, t), t)
        sa[...] = mm1(lax.div(nxt, STEPS), 2 * lax.rem(nxt, STEPS))
        acc[ch] += first + mm2(weigh(sb, ch, t + 1), t + 1)

        def when(n, *jobs):
            @pl.when(i == n)
            def _():
                for job in jobs:
                    job()

        when(3, lambda: swap(0).start())
        when(4, lambda: begin(0))
        when(6, lambda: outs[0].stage2())
        when(7, lambda: swap(1).start())
        when(8, lambda: begin(1), lambda: outs[0].stage3())
        when(10, lambda: outs[1].stage2(), lambda: outs[0].stage4())
        return carry

    lax.fori_loop(0, NCH * STEPS, step, 0)
    swap(2).start()
    outs[1].stage3()
    from_chips(pots2, pot2_s, pot2_r)
    for q in range(CHIPS):
        listpot_ref[q * BLOCKS : (q + 1) * BLOCKS, :] = pots2[q, 0:BLOCKS, :] * LN2
    begin(2)
    outs[1].stage4()
    outs[2].stage2()
    outs[2].stage3()
    outs[2].stage4()
    for ch in range(NCH):
        keep(ch).wait()
        outs[ch].finish()


def local(key_rows, centroids):
    vmem = pl.BlockSpec(memory_space=pltpu.VMEM)
    dma = pltpu.SemaphoreType.DMA
    small = (8, 128)
    new, row_pot, list_pot = pl.pallas_call(
        kernel,
        out_shape=(
            jax.ShapeDtypeStruct((NL, D), bf16),
            jax.ShapeDtypeStruct(small, f32),
            jax.ShapeDtypeStruct((NL // 128, 128), f32),
        ),
        in_specs=[vmem, vmem],
        out_specs=(pl.BlockSpec(memory_space=pl.ANY), vmem, vmem),
        scratch_shapes=[
            pltpu.VMEM((NT, NK, W), f32),
            pltpu.VMEM((NK, 128), f32),
            pltpu.VMEM((NK, 128), f32),
            pltpu.VMEM((NK, 128), f32),
            pltpu.VMEM((NT, 8, W), f32),
            pltpu.VMEM((CHIPS, 2, *small), f32),
            pltpu.VMEM((CHIPS, *small), f32),
            pltpu.VMEM((CHIPS, *small), f32),
            pltpu.VMEM((CHIPS, *small), f32),
            pltpu.VMEM((N_LIST, 2, *small), f32),
            pltpu.VMEM((N_LIST, *small), f32),
            pltpu.VMEM((N_ROW, 2, *small), f32),
            pltpu.VMEM((N_ROW, *small), f32),
            pltpu.VMEM((CHIPS, *small), f32),
            pltpu.VMEM((CHIPS, NK, D), bf16),
            pltpu.VMEM((1, CHIPS * NK), f32),
            pltpu.VMEM((SHARE, 128), f32),
            pltpu.VMEM((LB, KT), f32),
            pltpu.VMEM((LB, KT), f32),
            pltpu.VMEM((NCH, LB, D), f32),
            pltpu.VMEM((NCH, LB // 2, D), f32),
            pltpu.VMEM((NCH, LB // 2, D), bf16),
            dma((N_LIST,)), dma((N_LIST,)), dma((N_LIST,)), dma((N_LIST,)),
            dma((N_ROW,)), dma((N_ROW,)), dma((N_ROW,)), dma((N_ROW,)),
            dma((CHIPS,)), dma((CHIPS,)), dma((CHIPS,)), dma((CHIPS,)), dma((CHIPS,)), dma((CHIPS,)),
            dma((9,)), dma((9,)), dma((NCH,)), dma((NCH,)), dma((NCH, 20)), dma((NCH, 20)), dma((NCH,)),
        ],
        compiler_params=pltpu.CompilerParams(
            collective_id=0, has_side_effects=True, vmem_limit_bytes=60 * 2**20
        ),
        name="sinkhorn",
    )(key_rows, centroids)
    return new, row_pot.reshape(NK), list_pot.reshape(NL)


def solution(mesh):
    return jax.shard_map(
        local,
        mesh=mesh,
        in_specs=(P("row", None), P("list", None)),
        out_specs=(P("list", None), P("row"), P("list")),
        check_vma=False,
    )
```

time: 521 us -> 113 us (0.22)
  blocking collectives: 432 us -> 0 us
  Pallas kernels: 0 us -> 107 us
  matrix products: 59.7 us -> 0 us
  other arithmetic: 20.6 us -> 0 us
    psum x5 -> x0, blocking collectives: 274 us -> none  [the longest x1 136 us: local(): lax.psum(lax.dot_general(weights, key_rows, (((0,), (0,)), ((), ())), pre...]
    pmax x4 -> x0, blocking collectives: 158 us -> none  [the longest x2 117 us: col_update(): highest = lax.pmax(peak, 'row')]
    pallas_call x0 -> x1, Pallas kernels: none -> 107 us  [local(): pl.pallas_call(kernel, out_shape=(jax.ShapeDtypeStruct((NL, D), bf16), ja...]
    dot_general x25 -> x0, matrix products: 59.7 us -> none  [the longest x24 47 us: scored_tile(): lax.dot_general(key_rows, cent_tile, (((1,), (1,)), ((), ())), preferred_...]
    reduce_sum x24 -> x0, other arithmetic: 20.3 us -> none  [the longest x12 10.6 us: column_stats(): return (top, jnp.sum(jnp.exp(scored - top[None, :]), axis=0))]
where the time goes in v1:
time: 113 us
  Pallas kernels  107 us (95%)
  local copies, waits for them, and re-layouts  4.97 us (4%)
    pallas_call x1, Pallas kernels, local(): pl.pallas_call(kernel, out_shape=(jax.ShapeDtypeStruct((NL, D), bf16), ja...  107 us
    unnamed x7, local copies, waits for them, and re-layouts  4.97 us

profile of v1, /device:TPU:1, one launch (start us, length us, event | category | flops | bytes accessed | tf_op | source)
XLA Modules:
  0.0 112.7 jit_solution(8169916576013924773)
XLA Ops:
  0.6 107.0 %sinkhorn.1 = (bf16[6144,256]{1,0:T(8,128)(2,1)}, f32[8,128]{1,0:T(8,128)}, f32[48,128]{1,0:T(8,128)}) custom-call(bf16[1024,256]{1,0:T(8,128)(2,1)} %keys.1, bf16[6144,256]{1,0:T(8,128)(2,1)} %cents.1), custom_call_target="tpu_custom_call" | custom-call | tf_op jit(solution)/shard_map/sinkhorn/pallas_call | solution.py:466
  107.7 0.0 copy-start.1
  107.7 0.0 copy-start
  107.7 3.8 %copy.8 = bf16[6144,256]{1,0:T(8,128)(2,1)} copy(bf16[6144,256]{1,0:T(8,128)(2,1)} %get-tuple-element.12) | data formatting | bytes 6291456
  111.4 0.0 copy-done.1
  111.4 0.6 copy.9
  112.0 0.0 copy-done
  112.0 0.6 copy.10
Async XLA Ops:
  107.7 3.8 %copy-start.1 = (f32[8,128]{1,0:T(8,128)S(1)}, f32[8,128]{1,0:T(8,128)}, u32[]{:S(2)}) copy-start(f32[8,128]{1,0:T(8,128)} %get-tuple-element.7) | copy-start | bytes 12292
  107.7 4.4 %copy-start = (f32[48,128]{1,0:T(8,128)S(1)}, f32[48,128]{1,0:T(8,128)}, u32[]{:S(2)}) copy-start(f32[48,128]{1,0:T(8,128)} %get-tuple-element.8) | copy-start | bytes 73732

commit v2 on v1

v2 whole, which is shorter than its diff:
```python
import math

import jax
import jax.numpy as jnp
from jax import lax
from jax.experimental import pallas as pl
from jax.experimental.pallas import tpu as pltpu
from jax.sharding import PartitionSpec as P

MESH = pl.DeviceIdType.MESH
f32 = jnp.float32
bf16 = jnp.bfloat16
LOG2E = math.log2(math.e)
LN2 = math.log(2.0)

D = 256
SCALE = 2.0 / math.sqrt(D) * LOG2E
NK = 1024
NL = 6144
W = 512
NT = NL // W
N_ROW, N_LIST, SEATS = 16, 8, 8
SHARE = NL // SEATS
BLOCKS = SHARE // 128
LB = 256
NCH = SHARE // LB
KT = 1024
STEPS = SEATS * NK // (2 * KT)
LOG2_KEYS = math.log2(NK * N_ROW)
LOG2_LISTS = math.log2(NL * N_LIST)
NT_DIMS = (((1,), (1,)), ((), ()))
NN_DIMS = (((1,), (0,)), ((), ()))


def tree(op, xs):
    xs = list(xs)
    while len(xs) > 1:
        ys = [op(a, b) for a, b in zip(xs[::2], xs[1::2])]
        if len(xs) % 2:
            ys.append(xs[-1])
        xs = ys
    return xs[0]


def log2(x):
    return jnp.log(x) * LOG2E


def fold(op, x):
    return tree(op, [x[8 * i : 8 * i + 8] for i in range(x.shape[0] // 8)])


def row_pass(keys, cents, scores, peak, total, first, last):
    rb = 32

    def body(i, carry):
        for half in range(2):
            t = 2 * i + half
            lists = pl.ds(pl.multiple_of(t * W, W), W)
            s = lax.dot_general(keys[...], cents[lists, :], NT_DIMS, preferred_element_type=f32) * SCALE
            scores[t] = s
            for b in range(NK // rb):
                rows = slice(b * rb, (b + 1) * rb)
                xs = [s[rows, v * 128 : (v + 1) * 128] for v in range(W // 128)]
                before = peak[rows, :]
                top = jnp.maximum(before, tree(jnp.maximum, xs))
                sums = tree(jnp.add, [jnp.exp2(x - top) for x in xs])
                total[rows, :] = total[rows, :] * jnp.exp2(before - top) + sums
                peak[rows, :] = top
        return carry

    lax.fori_loop(first // 2, last // 2, body, 0)


def column_pass(scores, row_pot, stats, first, last):
    rb = 256

    def body(i, carry):
        for v in range(W // 128):
            lanes = slice(v * 128, (v + 1) * 128)
            tops = []
            for b in range(NK // rb):
                rows = slice(b * rb, (b + 1) * rb)
                x = scores[i, rows, lanes] + row_pot[rows, :]
                scores[i, rows, lanes] = x
                tops.append(fold(jnp.maximum, x))
            top = jnp.max(tree(jnp.maximum, tops), axis=0, keepdims=True)
            sums = []
            for b in range(NK // rb):
                rows = slice(b * rb, (b + 1) * rb)
                e = jnp.exp2(scores[i, rows, lanes] - top)
                scores[i, rows, lanes] = e
                sums.append(fold(jnp.add, e))
            total = jnp.sum(tree(jnp.add, sums), axis=0, keepdims=True)
            j = i * (W // 128) + v
            q, at = lax.div(j, BLOCKS), lax.rem(j, BLOCKS)
            stats[pl.ds(q, 1), 0, pl.ds(at, 1), :] = top[None]
            stats[pl.ds(q, 1), 1, pl.ds(at, 1), :] = total[None]
        return carry

    lax.fori_loop(first, last, body, 0)


def row_sums(scores, gain, total):
    rb, group = 64, 4

    def body(i, carry):
        def at(b):
            return pl.ds(pl.multiple_of(i * rb + 8 * b, 8), 8)

        def inner(c, accs):
            accs = list(accs)
            for t in range(group):
                for v in range(W // 128):
                    lanes = slice(v * 128, (v + 1) * 128)
                    g = gain[c * group + t, :, lanes]
                    for b in range(rb // 8):
                        accs[b] = accs[b] + scores[c * group + t, at(b), lanes] * g
            return tuple(accs)

        zero = jnp.zeros((8, 128), f32)
        accs = lax.fori_loop(0, NT // group, inner, (zero,) * (rb // 8))
        for b in range(rb // 8):
            total[at(b), :] = accs[b]
        return carry

    lax.fori_loop(0, NK // rb, body, 0)


def column_sums(scores, factor, sums):
    rb = 128

    def body(i, carry):
        accs = [[] for _ in range(W // 128)]
        for b in range(NK // rb):
            rows = slice(b * rb, (b + 1) * rb)
            u = factor[rows, :]
            for v in range(W // 128):
                part = fold(jnp.add, scores[i, rows, v * 128 : (v + 1) * 128] * u)
                accs[v] = part if b == 0 else accs[v] + part
        for v in range(W // 128):
            j = i * (W // 128) + v
            q, at = lax.div(j, BLOCKS), lax.rem(j, BLOCKS)
            sums[pl.ds(q, 1), pl.ds(at, 1), :] = jnp.sum(accs[v], axis=0, keepdims=True)[None]
        return carry

    lax.fori_loop(0, NT, body, 0)


def spread(compact, n, out):
    for b in range(n):
        out[b * 128 : (b + 1) * 128, :] = jnp.broadcast_to(compact[b : b + 1, :], (128, 128)).T


def remote(src, dst, send, recv, target):
    return pltpu.make_async_remote_copy(
        src_ref=src, dst_ref=dst, send_sem=send, recv_sem=recv, device_id=target, device_id_type=MESH
    )


class Gather:
    def __init__(self, at, send, recv, y, x, core, own, ring=False):
        self.at, self.send, self.recv = at, send, recv
        self.y, self.x, self.core, self.own, self.ring = y, x, core, own, ring

        def device(dy, flip, of=core):
            return {"row": (lax.rem(y + dy + 4, 4) * 2 + (1 - x if flip else x)) * 2 + of}

        up, down, side = device(1, False), device(-1, False), device(0, True)
        self.other = device(0, False, 1 - core)
        self.moves = [
            (up, (0, False), (-1, False), None),
            (down, (0, False), (1, False), None),
            (up, (-1, False), (-2, False), 0),
            (down, (1, False), (2, False), 1),
            (side, (0, False), (0, True), None),
            (up, (0, True), (-1, True), None),
            (down, (0, True), (1, True), None),
            (side, (-2, False), (2, True), 0),
            (side, (2, False), (2, True), 1),
        ]
        self.used = range(4) if ring else range(9)

    def place(self, block, part, *of):
        dy, flip = block
        return self.at(lax.rem(self.y + dy + 4, 4), 1 - self.x if flip else self.x, part, *of)

    def source(self, block, part):
        return self.own if block == (0, False) else self.place(block, part)

    def copy(self, m):
        target, sent, _, part = self.moves[m]
        return remote(self.source(sent, part), self.place(sent, part), self.send.at[m], self.recv.at[m], target)

    def arrival(self, m):
        target, _, came, part = self.moves[m]
        place = self.place(came, part)
        return remote(place, place, self.send.at[m], self.recv.at[m], target)

    def brought(self, m):
        return ((0, False), None) if m == 9 else self.moves[m][2:]

    def hand(self, m):
        block, part = self.brought(m)
        return remote(
            self.source(block, part), self.place(block, part), self.send.at[10 + m], self.recv.at[10 + m], self.other
        )

    def handed(self, m):
        block, part = self.brought(m)
        place = self.place(block, part, 1 - self.core)
        return remote(place, place, self.send.at[10 + m], self.recv.at[10 + m], self.other)

    def take(self, m, *sends):
        if m in self.used:
            self.arrival(m).wait_recv()
            for n in sends:
                if n in self.used:
                    self.copy(n).start()
            self.hand(m).start()

    def stage1(self):
        for m in (0, 1, 4):
            if m in self.used:
                self.copy(m).start()
        self.hand(9).start()

    def stage2(self):
        self.take(0, 2)
        self.take(1, 3)
        self.take(4, 5, 6)

    def stage3(self):
        self.take(2, 7)
        self.take(3, 8)

    def stage4(self):
        for m in (5, 6, 7, 8):
            self.take(m)

    def arrive(self):
        for m in (*self.used, 9):
            self.handed(m).wait_recv()

    def sent(self):
        for m in self.used:
            self.copy(m).wait_send()
        for m in (*self.used, 9):
            self.hand(m).wait_send()


def kernel(
    keys, cents, new_ref, rowpot_ref, listpot_ref,
    scores, peak, total, row_pot, gain, gains, stats, sums, pots, pots2, from_list1, from_list3, from_row2, from_row4,
    row_all, keys_all, row_lanes, list_lanes, sa, sb, acc, give, came, done,
    list1_s, list1_r, list3_s, list3_r, row2_s, row2_r, row4_s, row4_r, pot_s, pot_r, pot2_s, pot2_r, all_s, all_r,
    keys_s, keys_r, twin_s, twin_r, out_s, out_r, here,
):
    row, lst = lax.axis_index("row"), lax.axis_index("list")
    core, x, y = lax.rem(row, 2), lax.rem(lax.div(row, 2), 2), lax.div(row, 4)
    seat = y * 2 + core

    def device(at, x):
        return (lax.div(at, 2) * 2 + x) * 2 + lax.rem(at, 2)

    def seat_of(device):
        return lax.div(device, 4) * 2 + lax.rem(device, 2)

    barrier = pltpu.get_barrier_semaphore()
    for k in range(1, N_ROW):
        pl.semaphore_signal(barrier, inc=1, device_id={"row": lax.rem(row + k, N_ROW)}, device_id_type=MESH)
    for k in range(1, N_LIST):
        pl.semaphore_signal(barrier, inc=1, device_id={"list": lax.rem(lst + k, N_LIST)}, device_id_type=MESH)
    stats[...] = jnp.zeros(stats.shape, f32)
    sums[...] = jnp.zeros(sums.shape, f32)
    peak[...] = jnp.full(peak.shape, -1e30, f32)
    total[...] = jnp.zeros(total.shape, f32)
    keys_all[seat] = keys[...]
    row_pass(keys, cents, scores, peak, total, 0, 4)
    pl.semaphore_wait(barrier, N_ROW + N_LIST - 2)

    def keys_at(y, x, part, of=core):
        at = y * 2 + of
        return keys_all.at[at] if part is None else keys_all.at[at, pl.ds(part * (NK // 2), NK // 2)]

    gather = Gather(keys_at, keys_s, keys_r, y, x, core, keys, ring=True)
    gather.stage1()
    sent = []

    def start(copies):
        for copy in copies:
            copy.start()
            sent.append(copy)

    def to_list(buf, send, recv):
        start(
            remote(buf.at[lst], buf.at[lst], send.at[k], recv.at[lst], {"list": lax.rem(lst + k, N_LIST)})
            for k in range(1, N_LIST)
        )

    def from_list(buf, send, recv):
        for k in range(1, N_LIST):
            src = lax.rem(lst + k, N_LIST)
            remote(buf.at[src], buf.at[src], send.at[k], recv.at[src], {"list": src}).wait_recv()

    def to_row(src_of, buf, send, recv):
        to = [lax.rem(row + k, N_ROW) for k in range(1, N_ROW)]
        start(
            remote(src_of.at[seat_of(t)], buf.at[row], send.at[k + 1], recv.at[row], {"row": t})
            for k, t in enumerate(to)
        )

    def from_row(buf, send, recv):
        for k in range(1, N_ROW):
            src = lax.rem(row + k, N_ROW)
            remote(buf.at[src], buf.at[src], send.at[k], recv.at[src], {"row": src}).wait_recv()

    def to_seats(buf, send, recv):
        to = [lax.rem(seat + k, SEATS) for k in range(1, SEATS)]
        start(
            remote(buf.at[seat], buf.at[seat], send.at[k + 1], recv.at[seat], {"row": device(t, x)})
            for k, t in enumerate(to)
        )

    def from_seats(buf, send, recv):
        for k in range(1, SEATS):
            src = lax.rem(seat + k, SEATS)
            remote(buf.at[src], buf.at[src], send.at[k], recv.at[src], {"row": device(src, x)}).wait_recv()

    row_pass(keys, cents, scores, peak, total, 4, NT)
    for b in range(NK // 128):
        rows = slice(b * 128, (b + 1) * 128)
        top = peak[rows, :].T
        best = jnp.max(top, axis=0, keepdims=True)
        part = jnp.sum(total[rows, :].T * jnp.exp2(top - best), axis=0, keepdims=True)
        from_list1[lst, 0, b : b + 1, :] = best
        from_list1[lst, 1, b : b + 1, :] = part
    to_list(from_list1, list1_s, list1_r)
    from_list(from_list1, list1_s, list1_r)
    best = tree(jnp.maximum, [from_list1[k, 0] for k in range(N_LIST)])
    whole = tree(jnp.add, [from_list1[k, 1] * jnp.exp2(from_list1[k, 0] - best) for k in range(N_LIST)])
    row1 = -LOG2_KEYS - (best + log2(whole))
    spread(row1, NK // 128, row_pot)

    column_pass(scores, row_pot, stats, 0, 4)
    gather.stage2()
    column_pass(scores, row_pot, stats, 4, NT)
    from_row2[row] = stats[seat]
    to_row(stats, from_row2, row2_s, row2_r)
    from_row(from_row2, row2_s, row2_r)
    best = tree(jnp.maximum, [from_row2[k, 0] for k in range(N_ROW)])
    whole = tree(jnp.add, [from_row2[k, 1] * jnp.exp2(from_row2[k, 0] - best) for k in range(N_ROW)])
    pots[seat] = -LOG2_LISTS - (best + log2(whole))
    to_seats(pots, pot_s, pot_r)
    gather.stage3()
    from_seats(pots, pot_s, pot_r)

    for q in range(SEATS):
        g = jnp.exp2(stats[q, 0] + pots[q])
        gains[q] = g
        for b in range(BLOCKS):
            j = q * BLOCKS + b
            v = j % (W // 128)
            gain[j // (W // 128), :, v * 128 : (v + 1) * 128] = jnp.broadcast_to(g[b : b + 1, :], (8, 128))
    row_sums(scores, gain, total)
    for b in range(NK // 128):
        from_list3[lst, b : b + 1, :] = jnp.sum(total[b * 128 : (b + 1) * 128, :].T, axis=0, keepdims=True)
    to_list(from_list3, list3_s, list3_r)
    from_list(from_list3, list3_s, list3_r)
    delta = -LOG2_KEYS - log2(tree(jnp.add, [from_list3[k] for k in range(N_LIST)]))
    row2 = row1 + delta
    row_all[seat] = row2
    to_seats(row_all, all_s, all_r)
    rowpot_ref[...] = row2 * LN2
    spread(jnp.exp2(delta), NK // 128, row_pot)

    column_sums(scores, row_pot, sums)
    for q in range(SEATS):
        sums[q] = sums[q] * gains[q]
    from_row4[row] = sums[seat]
    to_row(sums, from_row4, row4_s, row4_r)
    gather.arrive()
    from_seats(row_all, all_s, all_r)
    for q in range(SEATS):
        for b in range(NK // 128):
            row_lanes[:, (q * 8 + b) * 128 : (q * 8 + b + 1) * 128] = row_all[q, b : b + 1, :]
    from_row(from_row4, row4_s, row4_r)
    list2 = pots[seat] - LOG2_LISTS - log2(tree(jnp.add, [from_row4[k] for k in range(N_ROW)]))
    pots2[seat] = list2
    to_seats(pots2, pot2_s, pot2_r)
    spread(list2 + LOG2_LISTS, BLOCKS, list_lanes)

    half = LB // 2

    def chunk_at(ch):
        def at(y, x, part, of=core):
            base = pl.multiple_of((y * 2 + of) * SHARE + ch * LB + x * half, half)
            if part is None:
                return new_ref.at[pl.ds(base, half)]
            return new_ref.at[pl.ds(pl.multiple_of(base + part * (half // 2), half // 2), half // 2)]

        return at

    outs = [Gather(chunk_at(ch), out_s.at[ch], out_r.at[ch], y, x, core, done.at[ch]) for ch in range(NCH)]
    side = {"row": device(seat, 1 - x)}
    mine, theirs = pl.multiple_of(x * half, half), pl.multiple_of((1 - x) * half, half)

    def swap(ch):
        return remote(give.at[ch], came.at[ch], twin_s.at[ch], twin_r.at[ch], side)

    def begin_swap(ch):
        give[ch] = acc[ch, pl.ds(theirs, half), :].astype(bf16)
        swap(ch).start()

    def keep(ch):
        return pltpu.make_async_copy(done.at[ch], chunk_at(ch)(y, x, None), here.at[ch])

    def begin(ch):
        swap(ch).wait()
        done[ch] = (acc[ch, pl.ds(mine, half), :] + came[ch].astype(f32)).astype(bf16)
        outs[ch].stage1()
        keep(ch).start()

    def tile(t):
        return keys_all[lax.div(t * KT, NK)]

    def mm1(ch, t):
        c = cents[pl.ds(pl.multiple_of(seat * SHARE + ch * LB, LB), LB), :]
        return lax.dot_general(c, tile(t), NT_DIMS, preferred_element_type=f32)

    def weigh(s_ref, ch, t):
        c = list_lanes[pl.ds(pl.multiple_of(ch * LB, LB), LB), :]
        out = []
        for v in range(KT // 128):
            r = row_lanes[:, pl.ds(pl.multiple_of(t * KT + v * 128, 128), 128)]
            s = s_ref[:, v * 128 : (v + 1) * 128] * SCALE
            out.append(jnp.exp2((s + r) + c).astype(bf16))
        return jnp.concatenate(out, axis=1)

    def mm2(w, t):
        return lax.dot_general(w, tile(t), NN_DIMS, preferred_element_type=f32)

    acc[...] = jnp.zeros(acc.shape, f32)
    sa[...] = mm1(0, 0)

    def step(i, carry):
        ch, t = lax.div(i, STEPS), 2 * lax.rem(i, STEPS)
        nxt = lax.rem(i + 1, NCH * STEPS)
        sb[...] = mm1(ch, t + 1)
        first = mm2(weigh(sa, ch, t), t)
        sa[...] = mm1(lax.div(nxt, STEPS), 2 * lax.rem(nxt, STEPS))
        acc[ch] += first + mm2(weigh(sb, ch, t + 1), t + 1)

        def when(n, *jobs):
            @pl.when(i == n)
            def _():
                for job in jobs:
                    job()

        when(3, lambda: begin_swap(0))
        when(4, lambda: begin(0))
        when(6, lambda: outs[0].stage2())
        when(7, lambda: begin_swap(1))
        when(8, lambda: begin(1), lambda: outs[0].stage3())
        when(10, lambda: outs[1].stage2(), lambda: outs[0].stage4())
        return carry

    lax.fori_loop(0, NCH * STEPS, step, 0)
    begin_swap(2)
    outs[1].stage3()
    from_seats(pots2, pot2_s, pot2_r)
    for q in range(SEATS):
        listpot_ref[q * BLOCKS : (q + 1) * BLOCKS, :] = pots2[q, 0:BLOCKS, :] * LN2
    begin(2)
    outs[1].stage4()
    outs[2].stage2()
    outs[2].stage3()
    outs[2].stage4()
    for ch in range(NCH):
        keep(ch).wait()
        outs[ch].arrive()
        outs[ch].sent()
    gather.sent()
    for copy in sent:
        copy.wait_send()


def local(key_rows, centroids):
    vmem = pl.BlockSpec(memory_space=pltpu.VMEM)
    dma = pltpu.SemaphoreType.DMA
    small = (8, 128)
    new, row_pot, list_pot = pl.pallas_call(
        kernel,
        out_shape=(
            jax.ShapeDtypeStruct((NL, D), bf16),
            jax.ShapeDtypeStruct(small, f32),
            jax.ShapeDtypeStruct((NL // 128, 128), f32),
        ),
        in_specs=[vmem, vmem],
        out_specs=(pl.BlockSpec(memory_space=pl.ANY), vmem, vmem),
        scratch_shapes=[
            pltpu.VMEM((NT, NK, W), f32),
            pltpu.VMEM((NK, 128), f32),
            pltpu.VMEM((NK, 128), f32),
            pltpu.VMEM((NK, 128), f32),
            pltpu.VMEM((NT, 8, W), f32),
            pltpu.VMEM((SEATS, *small), f32),
            pltpu.VMEM((SEATS, 2, *small), f32),
            pltpu.VMEM((SEATS, *small), f32),
            pltpu.VMEM((SEATS, *small), f32),
            pltpu.VMEM((SEATS, *small), f32),
            pltpu.VMEM((N_LIST, 2, *small), f32),
            pltpu.VMEM((N_LIST, *small), f32),
            pltpu.VMEM((N_ROW, 2, *small), f32),
            pltpu.VMEM((N_ROW, *small), f32),
            pltpu.VMEM((SEATS, *small), f32),
            pltpu.VMEM((SEATS, NK, D), bf16),
            pltpu.VMEM((1, SEATS * NK), f32),
            pltpu.VMEM((SHARE, 128), f32),
            pltpu.VMEM((LB, KT), f32),
            pltpu.VMEM((LB, KT), f32),
            pltpu.VMEM((NCH, LB, D), f32),
            pltpu.VMEM((NCH, LB // 2, D), bf16),
            pltpu.VMEM((NCH, LB // 2, D), bf16),
            pltpu.VMEM((NCH, LB // 2, D), bf16),
            dma((N_LIST,)), dma((N_LIST,)), dma((N_LIST,)), dma((N_LIST,)),
            dma((N_ROW,)), dma((N_ROW,)), dma((N_ROW,)), dma((N_ROW,)),
            dma((SEATS,)), dma((SEATS,)), dma((SEATS,)), dma((SEATS,)), dma((SEATS,)), dma((SEATS,)),
            dma((20,)), dma((20,)), dma((NCH,)), dma((NCH,)), dma((NCH, 20)), dma((NCH, 20)), dma((NCH,)),
        ],
        compiler_params=pltpu.CompilerParams(
            collective_id=0, has_side_effects=True, vmem_limit_bytes=60 * 2**20
        ),
        name="sinkhorn",
    )(key_rows, centroids)
    return new, row_pot.reshape(NK), list_pot.reshape(NL)


def solution(mesh):
    return jax.shard_map(
        local,
        mesh=mesh,
        in_specs=(P("row", None), P("list", None)),
        out_specs=(P("list", None), P("row"), P("list")),
        check_vma=False,
    )
```

time: 113 us -> 97.6 us (0.86)
  Pallas kernels: 107 us -> 91.9 us
    pallas_call x1, Pallas kernels: 107 us -> 91.9 us  [local(): pl.pallas_call(kernel, out_shape=(jax.ShapeDtypeStruct((NL, D), bf16), ja...]
where the time goes in v2:
time: 97.6 us; the launch traced here: 97.5 us
  Pallas kernels  91.9 us (94%)
  local copies, waits for them, and re-layouts  4.97 us (5%)
    pallas_call x1, Pallas kernels, local(): pl.pallas_call(kernel, out_shape=(jax.ShapeDtypeStruct((NL, D), bf16), ja...  91.9 us
    unnamed x7, local copies, waits for them, and re-layouts  4.97 us

profile of v2, /device:TPU:1, one launch (start us, length us, event | category | flops | bytes accessed | tf_op | source)
XLA Modules:
  0.0 97.5 jit_solution(11917463310781752640)
XLA Ops:
  0.6 91.9 %sinkhorn.1 = (bf16[6144,256]{1,0:T(8,128)(2,1)}, f32[8,128]{1,0:T(8,128)}, f32[48,128]{1,0:T(8,128)}) custom-call(bf16[1024,256]{1,0:T(8,128)(2,1)} %keys.1, bf16[6144,256]{1,0:T(8,128)(2,1)} %cents.1), custom_call_target="tpu_custom_call" | custom-call | tf_op jit(solution)/shard_map/sinkhorn/pallas_call | solution.py:492
  92.5 0.0 copy-start.1
  92.5 0.0 copy-start
  92.5 3.8 %copy.8 = bf16[6144,256]{1,0:T(8,128)(2,1)} copy(bf16[6144,256]{1,0:T(8,128)(2,1)} %get-tuple-element.12) | data formatting | bytes 6291456
  96.3 0.0 copy-done.1
  96.3 0.6 copy.9
  96.9 0.0 copy-done
  96.9 0.6 copy.10
Async XLA Ops:
  92.5 3.8 %copy-start.1 = (f32[8,128]{1,0:T(8,128)S(1)}, f32[8,128]{1,0:T(8,128)}, u32[]{:S(2)}) copy-start(f32[8,128]{1,0:T(8,128)} %get-tuple-element.7) | copy-start | bytes 12292
  92.5 4.4 %copy-start = (f32[48,128]{1,0:T(8,128)S(1)}, f32[48,128]{1,0:T(8,128)}, u32[]{:S(2)}) copy-start(f32[48,128]{1,0:T(8,128)} %get-tuple-element.8) | copy-start | bytes 73732

commit v3 on v2

--- a/solution.py
+++ b/solution.py
@@ -252,7 +252,7 @@
 def kernel(
     keys, cents, new_ref, rowpot_ref, listpot_ref,
     scores, peak, total, row_pot, gain, gains, stats, sums, pots, pots2, from_list1, from_list3, from_row2, from_row4,
-    row_all, keys_all, row_lanes, list_lanes, sa, sb, acc, give, came, done,
+    row_all, keys_all, row_lanes, list_lanes, sa, sb, wa, wb, acc, give, came, done,
     list1_s, list1_r, list3_s, list3_r, row2_s, row2_r, row4_s, row4_r, pot_s, pot_r, pot2_s, pot2_r, all_s, all_r,
     keys_s, keys_r, twin_s, twin_r, out_s, out_r, here,
 ):
@@ -428,28 +428,31 @@
         c = cents[pl.ds(pl.multiple_of(seat * SHARE + ch * LB, LB), LB), :]
         return lax.dot_general(c, tile(t), NT_DIMS, preferred_element_type=f32)
 
-    def weigh(s_ref, ch, t):
+    def mm2(w_ref, t):
+        return lax.dot_general(w_ref[...], tile(t), NN_DIMS, preferred_element_type=f32)
+
+    def weigh(s_ref, w_ref, ch, t):
         c = list_lanes[pl.ds(pl.multiple_of(ch * LB, LB), LB), :]
-        out = []
         for v in range(KT // 128):
+            lanes = slice(v * 128, (v + 1) * 128)
             r = row_lanes[:, pl.ds(pl.multiple_of(t * KT + v * 128, 128), 128)]
-            s = s_ref[:, v * 128 : (v + 1) * 128] * SCALE
-            out.append(jnp.exp2((s + r) + c).astype(bf16))
-        return jnp.concatenate(out, axis=1)
-
-    def mm2(w, t):
-        return lax.dot_general(w, tile(t), NN_DIMS, preferred_element_type=f32)
+            w_ref[:, lanes] = jnp.exp2((s_ref[:, lanes] * SCALE + r) + c).astype(bf16)
 
     acc[...] = jnp.zeros(acc.shape, f32)
+    wb[...] = jnp.zeros(wb.shape, bf16)
     sa[...] = mm1(0, 0)
 
     def step(i, carry):
         ch, t = lax.div(i, STEPS), 2 * lax.rem(i, STEPS)
-        nxt = lax.rem(i + 1, NCH * STEPS)
+        nxt, prv = lax.rem(i + 1, NCH * STEPS), lax.rem(i + NCH * STEPS - 1, NCH * STEPS)
+        before = mm2(wb, 2 * lax.rem(prv, STEPS) + 1)
         sb[...] = mm1(ch, t + 1)
-        first = mm2(weigh(sa, ch, t), t)
+        weigh(sa, wa, ch, t)
+        acc[lax.div(prv, STEPS)] += before
+        now = mm2(wa, t)
         sa[...] = mm1(lax.div(nxt, STEPS), 2 * lax.rem(nxt, STEPS))
-        acc[ch] += first + mm2(weigh(sb, ch, t + 1), t + 1)
+        weigh(sb, wb, ch, t + 1)
+        acc[ch] += now
 
         def when(n, *jobs):
             @pl.when(i == n)
@@ -457,23 +460,25 @@
                 for job in jobs:
                     job()
 
-        when(3, lambda: begin_swap(0))
-        when(4, lambda: begin(0))
-        when(6, lambda: outs[0].stage2())
-        when(7, lambda: begin_swap(1))
-        when(8, lambda: begin(1), lambda: outs[0].stage3())
-        when(10, lambda: outs[1].stage2(), lambda: outs[0].stage4())
+        when(STEPS, lambda: begin_swap(0))
+        when(2 * STEPS - 1, lambda: begin(0))
+        when(2 * STEPS, lambda: begin_swap(1))
+        when(3 * STEPS - 1, lambda: begin(1), outs[0].stage2)
         return carry
 
     lax.fori_loop(0, NCH * STEPS, step, 0)
+    acc[NCH - 1] += mm2(wb, SEATS * NK // KT - 1)
     begin_swap(2)
-    outs[1].stage3()
+    outs[0].stage3()
+    outs[1].stage2()
     from_seats(pots2, pot2_s, pot2_r)
     for q in range(SEATS):
         listpot_ref[q * BLOCKS : (q + 1) * BLOCKS, :] = pots2[q, 0:BLOCKS, :] * LN2
     begin(2)
+    outs[1].stage3()
+    outs[0].stage4()
+    outs[2].stage2()
     outs[1].stage4()
-    outs[2].stage2()
     outs[2].stage3()
     outs[2].stage4()
     for ch in range(NCH):
@@ -492,7 +497,7 @@
     new, row_pot, list_pot = pl.pallas_call(
         kernel,
         out_shape=(
-            jax.ShapeDtypeStruct((NL, D), bf16),
+            pltpu.VMEM((NL, D), bf16),
             jax.ShapeDtypeStruct(small, f32),
             jax.ShapeDtypeStruct((NL // 128, 128), f32),
         ),
@@ -519,6 +524,8 @@
             pltpu.VMEM((SHARE, 128), f32),
             pltpu.VMEM((LB, KT), f32),
             pltpu.VMEM((LB, KT), f32),
+            pltpu.VMEM((LB, KT), bf16),
+            pltpu.VMEM((LB, KT), bf16),
             pltpu.VMEM((NCH, LB, D), f32),
             pltpu.VMEM((NCH, LB // 2, D), bf16),
             pltpu.VMEM((NCH, LB // 2, D), bf16),
@@ -529,7 +536,7 @@
             dma((20,)), dma((20,)), dma((NCH,)), dma((NCH,)), dma((NCH, 20)), dma((NCH, 20)), dma((NCH,)),
         ],
         compiler_params=pltpu.CompilerParams(
-            collective_id=0, has_side_effects=True, vmem_limit_bytes=60 * 2**20
+            collective_id=0, has_side_effects=True, vmem_limit_bytes=44 * 2**20
         ),
         name="sinkhorn",
     )(key_rows, centroids)

time: 97.6 us -> 88.8 us (0.910)
  Pallas kernels: 91.9 us -> 82.2 us
    pallas_call x1, Pallas kernels: 91.9 us -> 82.2 us  [local(): pl.pallas_call(kernel, out_shape=(pltpu.VMEM((NL, D), bf16), jax.ShapeDty...]
where the time goes in v3:
time: 88.8 us; the launch traced here: 88.6 us
  Pallas kernels  82.2 us (93%)
  local copies, waits for them, and re-layouts  5.79 us (7%)
    pallas_call x1, Pallas kernels, local(): pl.pallas_call(kernel, out_shape=(pltpu.VMEM((NL, D), bf16), jax.ShapeDty...  82.2 us
    unnamed x7, local copies, waits for them, and re-layouts  5.79 us

profile of v3, /device:TPU:1, one launch (start us, length us, event | category | flops | bytes accessed | tf_op | source)
XLA Modules:
  0.0 88.6 jit_solution(9820619964384105286)
XLA Ops:
  0.6 0.0 copy-start
  0.6 1.9 %copy-done = bf16[6144,256]{1,0:T(8,128)(2,1)S(1)} copy-done((bf16[6144,256]{1,0:T(8,128)(2,1)S(1)}, bf16[6144,256]{1,0:T(8,128)(2,1)}, u32[]{:S(2)}) %copy-start) | copy-done | bytes 3145752
  2.5 0.0 copy-start.1
  2.5 1.0 %copy-done.1 = bf16[1024,256]{1,0:T(8,128)(2,1)S(1)} copy-done((bf16[1024,256]{1,0:T(8,128)(2,1)S(1)}, bf16[1024,256]{1,0:T(8,128)(2,1)}, u32[]{:S(2)}) %copy-start.1) | copy-done | bytes 524312
  3.6 82.2 %sinkhorn.1 = (bf16[6144,256]{1,0:T(8,128)(2,1)S(1)}, f32[8,128]{1,0:T(8,128)S(1)}, f32[48,128]{1,0:T(8,128)S(1)}) custom-call(bf16[1024,256]{1,0:T(8,128)(2,1)S(1)} %copy-done.1, bf16[6144,256]{1,0:T(8,128)(2,1)S(1)} %copy-done), custom_call_target="tpu_custom_call" | custom-call | tf_op jit(solution)/shard_map/sinkhorn/pallas_call | solution.py:497
  85.7 1.7 %copy.8 = bf16[6144,256]{1,0:T(8,128)(2,1)} copy(bf16[6144,256]{1,0:T(8,128)(2,1)S(1)} %get-tuple-element.9) | data formatting | bytes 6291456
  87.4 0.6 copy.9
  88.0 0.6 copy.10
Async XLA Ops:
  0.6 1.9 %copy-start = (bf16[6144,256]{1,0:T(8,128)(2,1)S(1)}, bf16[6144,256]{1,0:T(8,128)(2,1)}, u32[]{:S(2)}) copy-start(bf16[6144,256]{1,0:T(8,128)(2,1)} %cents.1) | copy-start | bytes 9437188
  2.5 1.0 %copy-start.1 = (bf16[1024,256]{1,0:T(8,128)(2,1)S(1)}, bf16[1024,256]{1,0:T(8,128)(2,1)}, u32[]{:S(2)}) copy-start(bf16[1024,256]{1,0:T(8,128)(2,1)} %keys.1) | copy-start | bytes 1572868

commit v4 on v3

v4 whole, which is shorter than its diff:
```python
import math

import jax
import jax.numpy as jnp
from jax import lax
from jax.experimental import pallas as pl
from jax.experimental.pallas import tpu as pltpu
from jax.sharding import PartitionSpec as P

MESH = pl.DeviceIdType.MESH
f32 = jnp.float32
bf16 = jnp.bfloat16
LOG2E = math.log2(math.e)
LN2 = math.log(2.0)

D = 256
SCALE = 2.0 / math.sqrt(D) * LOG2E
NK = 1024
NL = 6144
W = 512
NT = NL // W
HALF = NK // 2
N_ROW, N_LIST, SEATS = 16, 8, 8
SHARE = NL // SEATS
BLOCKS = SHARE // 128
LB = SHARE // 2
PIECE = 128
NCH = LB // PIECE
VMEM = 243 * 2**18
KT = 1024
STEPS = SEATS * NK // (2 * KT)
LOG2_KEYS = math.log2(NK * N_ROW)
LOG2_LISTS = math.log2(NL * N_LIST)
NT_DIMS = (((1,), (1,)), ((), ()))
NN_DIMS = (((1,), (0,)), ((), ()))


def tree(op, xs):
    xs = list(xs)
    while len(xs) > 1:
        ys = [op(a, b) for a, b in zip(xs[::2], xs[1::2])]
        if len(xs) % 2:
            ys.append(xs[-1])
        xs = ys
    return xs[0]


def log2(x):
    return jnp.log(x) * LOG2E


def fold(op, x):
    return tree(op, [x[8 * i : 8 * i + 8] for i in range(x.shape[0] // 8)])


def score_tile(keys, cents, scores, peak, i, half, part):
    rb = 32
    lists = pl.ds(pl.multiple_of((2 * i + half) * W, W), W)
    mine = keys[part * HALF : (part + 1) * HALF, :]
    s = lax.dot_general(mine, cents[lists, :], NT_DIMS, preferred_element_type=f32) * SCALE
    scores[i, half, part] = s
    for b in range(HALF // rb):
        rows = slice(part * HALF + b * rb, part * HALF + (b + 1) * rb)
        xs = [s[b * rb : (b + 1) * rb, v * 128 : (v + 1) * 128] for v in range(W // 128)]
        peak[rows, :] = jnp.maximum(peak[rows, :], tree(jnp.maximum, xs))


def sum_tile(scores, peak, total, i, half, part):
    rb = 32
    for b in range(HALF // rb):
        rows = slice(part * HALF + b * rb, part * HALF + (b + 1) * rb)
        top = peak[rows, :]
        xs = [scores[i, half, part, b * rb : (b + 1) * rb, v * 128 : (v + 1) * 128] for v in range(W // 128)]
        total[rows, :] += tree(jnp.add, [jnp.exp2(x - top) for x in xs])


def row_pass(work):
    def body(i, carry):
        for half in range(2):
            for step in work:
                step(i, half)
        return carry

    lax.fori_loop(0, NT // 2, body, 0)


def column_pass(scores, row_pot, stats, part, first, last):
    rb = 64
    columns = [(half, v) for half in range(2) for v in range(W // 128)]

    def body(i, carry):
        def at(n, b):
            half, v = columns[n]
            return i, half, part, slice(b * rb, (b + 1) * rb), slice(v * 128, (v + 1) * 128)

        top = None
        for n in range(len(columns) + 1):
            peaks = sums = None
            for b in range(HALF // rb):
                if n < len(columns):
                    x = scores[at(n, b)] + row_pot[part * HALF + b * rb : part * HALF + (b + 1) * rb, :]
                    scores[at(n, b)] = x
                    x = fold(jnp.maximum, x)
                    peaks = x if b == 0 else jnp.maximum(peaks, x)
                if n > 0:
                    e = jnp.exp2(scores[at(n - 1, b)] - top)
                    scores[at(n - 1, b)] = e
                    e = fold(jnp.add, e)
                    sums = e if b == 0 else sums + e
            if n > 0:
                j = i * len(columns) + n - 1
                q, row = lax.div(j, BLOCKS), lax.rem(j, BLOCKS)
                stats[part, pl.ds(q, 1), 0, pl.ds(row, 1), :] = top[None]
                stats[part, pl.ds(q, 1), 1, pl.ds(row, 1), :] = jnp.sum(sums, axis=0, keepdims=True)[None]
            if n < len(columns):
                top = jnp.max(peaks, axis=0, keepdims=True)
        return carry

    lax.fori_loop(first, last, body, 0)


def row_sums(scores, gain, total, part):
    rb, group = 64, 4

    def body(i, carry):
        def at(b):
            return pl.ds(pl.multiple_of(i * rb + 8 * b, 8), 8)

        def out(b):
            return pl.ds(pl.multiple_of(part * HALF + i * rb + 8 * b, 8), 8)

        def inner(c, accs):
            accs = list(accs)
            for t in range(group):
                for v in range(W // 128):
                    lanes = slice(v * 128, (v + 1) * 128)
                    g = gain[part, c * group + t, :, lanes]
                    for b in range(rb // 8):
                        accs[b] = accs[b] + scores[c * (group // 2) + t // 2, t % 2, part, at(b), lanes] * g
            return tuple(accs)

        zero = jnp.zeros((8, 128), f32)
        accs = lax.fori_loop(0, NT // group, inner, (zero,) * (rb // 8))
        for b in range(rb // 8):
            total[out(b), :] = accs[b]
        return carry

    lax.fori_loop(0, HALF // rb, body, 0)


def spread(compact, n, out, first=0):
    for b in range(n):
        out[first + b * 128 : first + (b + 1) * 128, :] = jnp.broadcast_to(compact[b : b + 1, :], (128, 128)).T


def remote(src, dst, send, recv, target):
    return pltpu.make_async_remote_copy(
        src_ref=src, dst_ref=dst, send_sem=send, recv_sem=recv, device_id=target, device_id_type=MESH
    )


class Gather:
    def __init__(self, at, send, recv, y, x, core, own, ring=False):
        self.at, self.send, self.recv = at, send, recv
        self.y, self.x, self.core, self.own, self.ring = y, x, core, own, ring

        def device(dy, flip, of=core):
            return {"row": (lax.rem(y + dy + 4, 4) * 2 + (1 - x if flip else x)) * 2 + of}

        up, down, side = device(1, False), device(-1, False), device(0, True)
        self.other = device(0, False, 1 - core)
        self.moves = [
            (up, (0, False), (-1, False), None),
            (down, (0, False), (1, False), None),
            (up, (-1, False), (-2, False), 0),
            (down, (1, False), (2, False), 1),
            (side, (0, False), (0, True), None),
            (up, (0, True), (-1, True), None),
            (down, (0, True), (1, True), None),
            (side, (-2, False), (2, True), 0),
            (side, (2, False), (2, True), 1),
        ]
        self.used = range(4) if ring else range(9)

    def place(self, block, part, *of):
        dy, flip = block
        return self.at(lax.rem(self.y + dy + 4, 4), 1 - self.x if flip else self.x, part, *of)

    def source(self, block, part):
        return self.own if block == (0, False) else self.place(block, part)

    def copy(self, m):
        target, sent, _, part = self.moves[m]
        return remote(self.source(sent, part), self.place(sent, part), self.send.at[m], self.recv.at[m], target)

    def arrival(self, m):
        target, _, came, part = self.moves[m]
        place = self.place(came, part)
        return remote(place, place, self.send.at[m], self.recv.at[m], target)

    def brought(self, m):
        return ((0, False), None) if m == 9 else self.moves[m][2:]

    def hand(self, m):
        block, part = self.brought(m)
        return remote(
            self.source(block, part), self.place(block, part), self.send.at[10 + m], self.recv.at[10 + m], self.other
        )

    def handed(self, m):
        block, part = self.brought(m)
        place = self.place(block, part, 1 - self.core)
        return remote(place, place, self.send.at[10 + m], self.recv.at[10 + m], self.other)

    def take(self, m, *sends):
        if m in self.used:
            self.arrival(m).wait_recv()
            for n in sends:
                if n in self.used:
                    self.copy(n).start()
            self.hand(m).start()

    def stage1(self):
        for m in (0, 1, 4):
            if m in self.used:
                self.copy(m).start()
        self.hand(9).start()

    def stage2(self):
        self.take(0, 2)
        self.take(1, 3)
        self.take(4, 5, 6)

    def stage3(self):
        self.take(2, 7)
        self.take(3, 8)

    def stage4(self):
        for m in (5, 6, 7, 8):
            self.take(m)

    def arrive(self):
        for m in (*self.used, 9):
            self.handed(m).wait_recv()

    def sent(self):
        for m in self.used:
            self.copy(m).wait_send()
        for m in (*self.used, 9):
            self.hand(m).wait_send()


def kernel(
    keys_hbm, cents_hbm, new_ref, rowpot_ref, listpot_ref,
    keys, cents, load, scores, peak, total, row_pot, row1, gain, stats, both, pots, pots2, from_list1, from_list3, from_row2,
    row_all, keys_all, row_lanes, list_lanes, sa, sb, wa, wb, acc, give, came, done, tsum, tmine, tcame,
    list1_s, list1_r, list3_s, list3_r, row2_s, row2_r, tsum_s, tsum_r, pot_s, pot_r, pot2_s, pot2_r, all_s, all_r,
    keys_s, keys_r, twin_s, twin_r, out_s, out_r, here,
):
    row, lst = lax.axis_index("row"), lax.axis_index("list")
    core, x, y = lax.rem(row, 2), lax.rem(lax.div(row, 2), 2), lax.div(row, 4)
    seat = y * 2 + core

    def device(at, x):
        return (lax.div(at, 2) * 2 + x) * 2 + lax.rem(at, 2)

    def seat_of(device):
        return lax.div(device, 4) * 2 + lax.rem(device, 2)

    barrier = pltpu.get_barrier_semaphore()
    for k in range(1, N_ROW):
        pl.semaphore_signal(barrier, inc=1, device_id={"row": lax.rem(row + k, N_ROW)}, device_id_type=MESH)
    for k in range(1, N_LIST):
        pl.semaphore_signal(barrier, inc=1, device_id={"list": lax.rem(lst + k, N_LIST)}, device_id_type=MESH)
    stats[...] = jnp.ones(stats.shape, f32)
    tmine[...] = jnp.zeros(tmine.shape, f32)
    pots2[...] = jnp.zeros(pots2.shape, f32)
    peak[...] = jnp.full(peak.shape, -1e30, f32)
    total[...] = jnp.zeros(total.shape, f32)
    loads = [
        pltpu.make_async_copy(keys_hbm, keys, load.at[0]),
        pltpu.make_async_copy(cents_hbm, cents, load.at[1]),
    ]
    for copy in loads:
        copy.start()

    def score(part):
        return lambda i, half: score_tile(keys, cents, scores, peak, i, half, part)

    def add(part):
        return lambda i, half: sum_tile(scores, peak, total, i, half, part)

    for copy in loads:
        copy.wait()
    keys_all[seat] = keys[...]
    row_pass([score(0)])
    row_pass([score(1), add(0)])
    pl.semaphore_wait(barrier, N_ROW + N_LIST - 2)

    def keys_at(y, x, part, of=core):
        at = y * 2 + of
        return keys_all.at[at] if part is None else keys_all.at[at, pl.ds(part * (NK // 2), NK // 2)]

    gather = Gather(keys_at, keys_s, keys_r, y, x, core, keys, ring=True)
    gather.stage1()
    sent = []

    def start(copies):
        for copy in copies:
            copy.start()
            sent.append(copy)

    def to_list(buf, send, recv):
        start(
            remote(buf.at[lst], buf.at[lst], send.at[k], recv.at[lst], {"list": lax.rem(lst + k, N_LIST)})
            for k in range(1, N_LIST)
        )

    def from_list(buf, send, recv):
        for k in range(1, N_LIST):
            src = lax.rem(lst + k, N_LIST)
            remote(buf.at[src], buf.at[src], send.at[k], recv.at[src], {"list": src}).wait_recv()

    def to_row(src_of, buf, send, recv):
        to = [lax.rem(row + k, N_ROW) for k in range(1, N_ROW)]
        start(
            remote(src_of.at[seat_of(t)], buf.at[row], send.at[k + 1], recv.at[row], {"row": t})
            for k, t in enumerate(to)
        )

    def from_row(buf, send, recv):
        for k in range(1, N_ROW):
            src = lax.rem(row + k, N_ROW)
            remote(buf.at[src], buf.at[src], send.at[k], recv.at[src], {"row": src}).wait_recv()

    def to_seats(buf, send, recv):
        to = [lax.rem(seat + k, SEATS) for k in range(1, SEATS)]
        start(
            remote(buf.at[seat], buf.at[seat], send.at[k + 1], recv.at[seat], {"row": device(t, x)})
            for k, t in enumerate(to)
        )

    def from_seats(buf, send, recv):
        for k in range(1, SEATS):
            src = lax.rem(seat + k, SEATS)
            remote(buf.at[src], buf.at[src], send.at[k], recv.at[src], {"row": device(src, x)}).wait_recv()

    n = HALF // 128

    def tell(part):
        for b in range(n):
            rows = slice(part * HALF + b * 128, part * HALF + (b + 1) * 128)
            top = peak[rows, :].T
            best = jnp.max(top, axis=0, keepdims=True)
            from_list1[part, lst, b : b + 1, :] = best
            from_list1[part, lst, n + b : n + b + 1, :] = jnp.sum(
                total[rows, :].T * jnp.exp2(top - best), axis=0, keepdims=True
            )
        to_list(from_list1.at[part], list1_s.at[part], list1_r.at[part])

    def learn(part):
        from_list(from_list1.at[part], list1_s.at[part], list1_r.at[part])
        best = tree(jnp.maximum, [from_list1[part, k, 0:n] for k in range(N_LIST)])
        whole = tree(
            jnp.add, [from_list1[part, k, n : 2 * n] * jnp.exp2(from_list1[part, k, 0:n] - best) for k in range(N_LIST)]
        )
        row1[part * n : (part + 1) * n, :] = -LOG2_KEYS - (best + log2(whole))
        spread(row1[part * n : (part + 1) * n, :], n, row_pot, part * HALF)

    tell(0)
    row_pass([add(1)])
    tell(1)

    learn(0)
    column_pass(scores, row_pot, stats, 0, 0, NT // 2)
    learn(1)
    column_pass(scores, row_pot, stats, 1, 0, NT // 2)
    for q in range(SEATS):
        best = jnp.maximum(stats[0, q, 0], stats[1, q, 0])
        both[q] = best + log2(tree(jnp.add, [stats[p, q, 1] * jnp.exp2(stats[p, q, 0] - best) for p in range(2)]))
    from_row2[row] = both[seat]
    to_row(both, from_row2, row2_s, row2_r)
    from_row(from_row2, row2_s, row2_r)
    best = tree(jnp.maximum, [from_row2[k] for k in range(N_ROW)])
    whole = tree(jnp.add, [jnp.exp2(from_row2[k] - best) for k in range(N_ROW)])
    pots[seat] = -LOG2_LISTS - (best + log2(whole))
    to_seats(pots, pot_s, pot_r)
    from_seats(pots, pot_s, pot_r)
    gather.stage2()

    for q in range(SEATS):
        for p in range(2):
            g = jnp.exp2(stats[p, q, 0] + pots[q])
            for b in range(BLOCKS):
                j = q * BLOCKS + b
                v = j % (W // 128)
                gain[p, j // (W // 128), :, v * 128 : (v + 1) * 128] = jnp.broadcast_to(g[b : b + 1, :], (8, 128))
    row_sums(scores, gain, total, 0)
    row_sums(scores, gain, total, 1)
    for b in range(NK // 128):
        from_list3[lst, b : b + 1, :] = jnp.sum(total[b * 128 : (b + 1) * 128, :].T, axis=0, keepdims=True)
    to_list(from_list3, list3_s, list3_r)
    from_list(from_list3, list3_s, list3_r)
    delta = -LOG2_KEYS - log2(tree(jnp.add, [from_list3[k] for k in range(N_LIST)]))
    row2 = row1[...] + delta
    row_all[seat] = row2
    to_seats(row_all, all_s, all_r)
    rowpot_ref[...] = row2 * LN2
    spread(pots[seat] + LOG2_LISTS, BLOCKS, list_lanes)
    acc[...] = jnp.zeros(acc.shape, f32)
    tsum[...] = jnp.zeros(tsum.shape, f32)
    gather.stage3()

    def base(block):
        return (block * x + (1 - block) * (1 - x)) * LB

    def piece_at(ch):
        def at(y, x, part, of=core):
            first = pl.multiple_of((y * 2 + of) * SHARE + x * LB + ch * PIECE, PIECE)
            if part is None:
                return new_ref.at[pl.ds(first, PIECE)]
            return new_ref.at[pl.ds(pl.multiple_of(first + part * (PIECE // 2), PIECE // 2), PIECE // 2)]

        return at

    outs = [Gather(piece_at(ch), out_s.at[ch], out_r.at[ch], y, x, core, done.at[ch]) for ch in range(NCH)]
    side = {"row": device(seat, 1 - x)}

    def swap(ch):
        return remote(give.at[ch], came.at[ch], twin_s.at[ch], twin_r.at[ch], side)

    def swap_sums(block):
        return remote(tmine.at[block], tcame.at[block], tsum_s.at[block], tsum_r.at[block], side)

    def sums(block):
        for b in range(NCH):
            rows = slice(b * 128, (b + 1) * 128)
            tmine[block, b : b + 1, :] = jnp.sum(tsum[block, rows, :].T, axis=0, keepdims=True)
        swap_sums(block).start()

    def hand_over():
        for ch in range(NCH):
            give[ch] = acc[0, ch * PIECE : (ch + 1) * PIECE, :].astype(bf16)
            swap(ch).start()
        sums(0)

    def keep(ch):
        return pltpu.make_async_copy(done.at[ch], piece_at(ch)(y, x, None), here.at[ch])

    def begin(ch):
        whole = tmine[1, ch : ch + 1, :] + tcame[0, ch : ch + 1, :]
        scale = jnp.broadcast_to(1.0 / whole, (PIECE, 128)).T
        swap(ch).wait()
        for v in range(D // 128):
            lanes = slice(v * 128, (v + 1) * 128)
            summed = acc[1, ch * PIECE : (ch + 1) * PIECE, lanes] + came[ch, :, lanes].astype(f32)
            done[ch, :, lanes] = (summed * scale).astype(bf16)
        outs[ch].stage1()
        keep(ch).start()

    def update(block, other):
        for b in range(NCH):
            at = pl.ds((block * x + (1 - block) * (1 - x)) * NCH + b, 1)
            whole = tmine[block, b : b + 1, :] + tcame[other, b : b + 1, :]
            pots2[seat, at, :] = pots[seat, at, :] - log2(whole)

    def tile(t):
        return keys_all[lax.div(t * KT, NK)]

    def mm1(block, t):
        c = cents[pl.ds(pl.multiple_of(seat * SHARE + base(block), LB), LB), :]
        return lax.dot_general(c, tile(t), NT_DIMS, preferred_element_type=f32)

    def mm2(w_ref, t):
        return lax.dot_general(w_ref[...], tile(t), NN_DIMS, preferred_element_type=f32)

    def weigh(s_ref, w_ref, block, t):
        c = list_lanes[pl.ds(pl.multiple_of(base(block), LB), LB), :]
        parts = []
        for v in range(KT // 128):
            lanes = slice(v * 128, (v + 1) * 128)
            r = row_lanes[:, pl.ds(pl.multiple_of(t * KT + v * 128, 128), 128)]
            e = jnp.exp2((s_ref[:, lanes] * SCALE + r) + c)
            w_ref[:, lanes] = e.astype(bf16)
            parts.append(e)
        tsum[block] += tree(jnp.add, parts)

    wb[...] = jnp.zeros(wb.shape, bf16)
    from_seats(row_all, all_s, all_r)
    gather.arrive()
    sa[...] = mm1(0, 0)
    for q in range(SEATS):
        for b in range(NK // 128):
            row_lanes[:, (q * 8 + b) * 128 : (q * 8 + b + 1) * 128] = row_all[q, b : b + 1, :]

    def step(i, carry):
        block, t = lax.div(i, STEPS), 2 * lax.rem(i, STEPS)
        nxt, prv = lax.rem(i + 1, 2 * STEPS), lax.rem(i + 2 * STEPS - 1, 2 * STEPS)
        before = mm2(wb, 2 * lax.rem(prv, STEPS) + 1)
        sb[...] = mm1(block, t + 1)
        weigh(sa, wa, block, t)
        acc[lax.div(prv, STEPS)] += before
        now = mm2(wa, t)
        sa[...] = mm1(lax.div(nxt, STEPS), 2 * lax.rem(nxt, STEPS))
        weigh(sb, wb, block, t + 1)
        acc[block] += now
        pl.when(i == STEPS)(hand_over)
        return carry

    lax.fori_loop(0, 2 * STEPS, step, 0)
    acc[1] += mm2(wb, SEATS * NK // KT - 1)
    sums(1)
    swap_sums(0).wait()
    for ch in range(NCH):
        begin(ch)
    swap_sums(1).wait()
    update(0, 1)
    update(1, 0)
    to_seats(pots2, pot2_s, pot2_r)
    outs[0].stage2()
    outs[1].stage2()
    outs[0].stage3()
    outs[2].stage2()
    outs[1].stage3()
    outs[0].stage4()
    outs[2].stage3()
    outs[1].stage4()
    outs[2].stage4()
    from_seats(pots2, pot2_s, pot2_r)
    for q in range(SEATS):
        listpot_ref[q * BLOCKS : (q + 1) * BLOCKS, :] = pots2[q, 0:BLOCKS, :] * LN2
    for ch in range(NCH):
        keep(ch).wait()
        outs[ch].arrive()
        outs[ch].sent()
    gather.sent()
    for copy in sent:
        copy.wait_send()


def local(key_rows, centroids):
    vmem = pl.BlockSpec(memory_space=pltpu.VMEM)
    dma = pltpu.SemaphoreType.DMA
    small = (8, 128)
    new, row_pot, list_pot = pl.pallas_call(
        kernel,
        out_shape=(
            pltpu.VMEM((NL, D), bf16),
            jax.ShapeDtypeStruct(small, f32),
            jax.ShapeDtypeStruct((NL // 128, 128), f32),
        ),
        in_specs=[pl.BlockSpec(memory_space=pltpu.HBM)] * 2,
        out_specs=(pl.BlockSpec(memory_space=pl.ANY), vmem, vmem),
        scratch_shapes=[
            pltpu.VMEM((NK, D), bf16),
            pltpu.VMEM((NL, D), bf16),
            dma((2,)),
            pltpu.VMEM((NT // 2, 2, 2, HALF, W), f32),
            pltpu.VMEM((NK, 128), f32),
            pltpu.VMEM((NK, 128), f32),
            pltpu.VMEM((NK, 128), f32),
            pltpu.VMEM(small, f32),
            pltpu.VMEM((2, NT, 8, W), f32),
            pltpu.VMEM((2, SEATS, 2, *small), f32),
            pltpu.VMEM((SEATS, *small), f32),
            pltpu.VMEM((SEATS, *small), f32),
            pltpu.VMEM((SEATS, *small), f32),
            pltpu.VMEM((2, N_LIST, *small), f32),
            pltpu.VMEM((N_LIST, *small), f32),
            pltpu.VMEM((N_ROW, *small), f32),
            pltpu.VMEM((SEATS, *small), f32),
            pltpu.VMEM((SEATS, NK, D), bf16),
            pltpu.VMEM((1, SEATS * NK), f32),
            pltpu.VMEM((SHARE, 128), f32),
            pltpu.VMEM((LB, KT), f32),
            pltpu.VMEM((LB, KT), f32),
            pltpu.VMEM((LB, KT), bf16),
            pltpu.VMEM((LB, KT), bf16),
            pltpu.VMEM((2, LB, D), f32),
            pltpu.VMEM((NCH, PIECE, D), bf16),
            pltpu.VMEM((NCH, PIECE, D), bf16),
            pltpu.VMEM((NCH, PIECE, D), bf16),
            pltpu.VMEM((2, LB, 128), f32),
            pltpu.VMEM((2, *small), f32),
            pltpu.VMEM((2, *small), f32),
            dma((2, N_LIST)), dma((2, N_LIST)), dma((N_LIST,)), dma((N_LIST,)),
            dma((N_ROW,)), dma((N_ROW,)), dma((2,)), dma((2,)),
            dma((SEATS,)), dma((SEATS,)), dma((SEATS,)), dma((SEATS,)), dma((SEATS,)), dma((SEATS,)),
            dma((20,)), dma((20,)), dma((NCH,)), dma((NCH,)), dma((NCH, 20)), dma((NCH, 20)), dma((NCH,)),
        ],
        compiler_params=pltpu.CompilerParams(
            collective_id=0, has_side_effects=True, vmem_limit_bytes=VMEM
        ),
        name="sinkhorn",
    )(key_rows, centroids)
    return new, row_pot.reshape(NK), list_pot.reshape(NL)


def solution(mesh):
    return jax.shard_map(
        local,
        mesh=mesh,
        in_specs=(P("row", None), P("list", None)),
        out_specs=(P("list", None), P("row"), P("list")),
        check_vma=False,
    )
```

time: 88.8 us -> 80.3 us (0.904)
  Pallas kernels: 82.2 us -> 76.7 us
  local copies, waits for them, and re-layouts: 5.79 us -> 2.88 us
    pallas_call x1, Pallas kernels: 82.2 us -> 76.7 us  [local(): pl.pallas_call(kernel, out_shape=(pltpu.VMEM((NL, D), bf16), jax.ShapeDty...]
    unnamed x7, local copies, waits for them, and re-layouts: 5.79 us -> 2.88 us
where the time goes in v4:
time: 80.3 us; the launch traced here: 80.2 us
  Pallas kernels  76.7 us (96%)
  local copies, waits for them, and re-layouts  2.88 us (4%)
    pallas_call x1, Pallas kernels, local(): pl.pallas_call(kernel, out_shape=(pltpu.VMEM((NL, D), bf16), jax.ShapeDty...  76.7 us
    unnamed x7, local copies, waits for them, and re-layouts  2.88 us

profile of v4, /device:TPU:1, one launch (start us, length us, event | category | flops | bytes accessed | tf_op | source)
XLA Modules:
  0.0 80.2 jit_solution(10980650864341556641)
XLA Ops:
  0.6 76.7 %sinkhorn.1 = (bf16[6144,256]{1,0:T(8,128)(2,1)S(1)}, f32[8,128]{1,0:T(8,128)}, f32[48,128]{1,0:T(8,128)}) custom-call(bf16[1024,256]{1,0:T(8,128)(2,1)} %keys_hbm.1, bf16[6144,256]{1,0:T(8,128)(2,1)} %cents_hbm.1), custom_call_target="tpu_custom_call" | custom-call | tf_op jit(solution)/shard_map/sinkhorn/pallas_call | solution.py:545
  77.3 0.0 copy-start.1
  77.3 0.0 copy-start
  77.3 1.7 %copy.8 = bf16[6144,256]{1,0:T(8,128)(2,1)} copy(bf16[6144,256]{1,0:T(8,128)(2,1)S(1)} %get-tuple-element.9) | data formatting | bytes 6291456
  79.0 0.0 copy-done.1
  79.0 0.6 copy.9
  79.6 0.0 copy-done
  79.6 0.6 copy.10
Async XLA Ops:
  77.3 1.7 %copy-start.1 = (f32[8,128]{1,0:T(8,128)S(1)}, f32[8,128]{1,0:T(8,128)}, u32[]{:S(2)}) copy-start(f32[8,128]{1,0:T(8,128)} %get-tuple-element.7) | copy-start | bytes 12292
  77.3 2.3 %copy-start = (f32[48,128]{1,0:T(8,128)S(1)}, f32[48,128]{1,0:T(8,128)}, u32[]{:S(2)}) copy-start(f32[48,128]{1,0:T(8,128)} %get-tuple-element.8) | copy-start | bytes 73732

commit v5 on v4

--- a/solution.py
+++ b/solution.py
@@ -21,14 +21,13 @@
 NT = NL // W
 HALF = NK // 2
 N_ROW, N_LIST, SEATS = 16, 8, 8
+FAR_FIRST = (*range(6, 11), 5, 11, 4, 12, 13, 3, 14, 2, 15, 1)
 SHARE = NL // SEATS
 BLOCKS = SHARE // 128
 LB = SHARE // 2
 PIECE = 128
 NCH = LB // PIECE
 VMEM = 243 * 2**18
-KT = 1024
-STEPS = SEATS * NK // (2 * KT)
 LOG2_KEYS = math.log2(NK * N_ROW)
 LOG2_LISTS = math.log2(NL * N_LIST)
 NT_DIMS = (((1,), (1,)), ((), ()))
@@ -239,8 +238,10 @@
         for m in (5, 6, 7, 8):
             self.take(m)
 
-    def arrive(self):
-        for m in (*self.used, 9):
+    def arrive(self, moves=range(10)):
+        for m in moves:
+            if m not in (*self.used, 9):
+                continue
             self.handed(m).wait_recv()
 
     def sent(self):
@@ -253,7 +254,7 @@
 def kernel(
     keys_hbm, cents_hbm, new_ref, rowpot_ref, listpot_ref,
     keys, cents, load, scores, peak, total, row_pot, row1, gain, stats, both, pots, pots2, from_list1, from_list3, from_row2,
-    row_all, keys_all, row_lanes, list_lanes, sa, sb, wa, wb, acc, give, came, done, tsum, tmine, tcame,
+    row_all, keys_all, row_lanes, list_lanes, late, wa, wb, acc, give, came, done, tsum, tmine, tcame,
     list1_s, list1_r, list3_s, list3_r, row2_s, row2_r, tsum_s, tsum_r, pot_s, pot_r, pot2_s, pot2_r, all_s, all_r,
     keys_s, keys_r, twin_s, twin_r, out_s, out_r, here,
 ):
@@ -290,64 +291,9 @@
     def add(part):
         return lambda i, half: sum_tile(scores, peak, total, i, half, part)
 
-    for copy in loads:
-        copy.wait()
-    keys_all[seat] = keys[...]
-    row_pass([score(0)])
-    row_pass([score(1), add(0)])
-    pl.semaphore_wait(barrier, N_ROW + N_LIST - 2)
-
-    def keys_at(y, x, part, of=core):
-        at = y * 2 + of
-        return keys_all.at[at] if part is None else keys_all.at[at, pl.ds(part * (NK // 2), NK // 2)]
-
-    gather = Gather(keys_at, keys_s, keys_r, y, x, core, keys, ring=True)
-    gather.stage1()
-    sent = []
-
-    def start(copies):
-        for copy in copies:
-            copy.start()
-            sent.append(copy)
-
-    def to_list(buf, send, recv):
-        start(
-            remote(buf.at[lst], buf.at[lst], send.at[k], recv.at[lst], {"list": lax.rem(lst + k, N_LIST)})
-            for k in range(1, N_LIST)
-        )
-
-    def from_list(buf, send, recv):
-        for k in range(1, N_LIST):
-            src = lax.rem(lst + k, N_LIST)
-            remote(buf.at[src], buf.at[src], send.at[k], recv.at[src], {"list": src}).wait_recv()
-
-    def to_row(src_of, buf, send, recv):
-        to = [lax.rem(row + k, N_ROW) for k in range(1, N_ROW)]
-        start(
-            remote(src_of.at[seat_of(t)], buf.at[row], send.at[k + 1], recv.at[row], {"row": t})
-            for k, t in enumerate(to)
-        )
-
-    def from_row(buf, send, recv):
-        for k in range(1, N_ROW):
-            src = lax.rem(row + k, N_ROW)
-            remote(buf.at[src], buf.at[src], send.at[k], recv.at[src], {"row": src}).wait_recv()
-
-    def to_seats(buf, send, recv):
-        to = [lax.rem(seat + k, SEATS) for k in range(1, SEATS)]
-        start(
-            remote(buf.at[seat], buf.at[seat], send.at[k + 1], recv.at[seat], {"row": device(t, x)})
-            for k, t in enumerate(to)
-        )
-
-    def from_seats(buf, send, recv):
-        for k in range(1, SEATS):
-            src = lax.rem(seat + k, SEATS)
-            remote(buf.at[src], buf.at[src], send.at[k], recv.at[src], {"row": device(src, x)}).wait_recv()
-
     n = HALF // 128
 
-    def tell(part):
+    def prepare(part):
         for b in range(n):
             rows = slice(part * HALF + b * 128, part * HALF + (b + 1) * 128)
             top = peak[rows, :].T
@@ -356,6 +302,64 @@
             from_list1[part, lst, n + b : n + b + 1, :] = jnp.sum(
                 total[rows, :].T * jnp.exp2(top - best), axis=0, keepdims=True
             )
+
+    for copy in loads:
+        copy.wait()
+    keys_all[seat] = keys[...]
+    row_pass([score(0)])
+    row_pass([score(1), add(0)])
+    prepare(0)
+    pl.semaphore_wait(barrier, N_ROW + N_LIST - 2)
+
+    def keys_at(y, x, part, of=core):
+        at = y * 2 + of
+        return keys_all.at[at] if part is None else keys_all.at[at, pl.ds(part * (NK // 2), NK // 2)]
+
+    gather = Gather(keys_at, keys_s, keys_r, y, x, core, keys, ring=True)
+    gather.stage1()
+    sent = []
+
+    def start(copies):
+        for copy in copies:
+            copy.start()
+            sent.append(copy)
+
+    def to_list(buf, send, recv):
+        start(
+            remote(buf.at[lst], buf.at[lst], send.at[k], recv.at[lst], {"list": lax.rem(lst + k, N_LIST)})
+            for k in (5, 3, 7, 1, 4, 6, 2)
+        )
+
+    def from_list(buf, send, recv):
+        for k in range(1, N_LIST):
+            src = lax.rem(lst + k, N_LIST)
+            remote(buf.at[src], buf.at[src], send.at[k], recv.at[src], {"list": src}).wait_recv()
+
+    def to_row(src_of, buf, send, recv):
+        to = [lax.rem(row + k, N_ROW) for k in FAR_FIRST]
+        start(
+            remote(src_of.at[seat_of(t)], buf.at[row], send.at[k + 1], recv.at[row], {"row": t})
+            for k, t in enumerate(to)
+        )
+
+    def from_row(buf, send, recv):
+        for k in range(1, N_ROW):
+            src = lax.rem(row + k, N_ROW)
+            remote(buf.at[src], buf.at[src], send.at[k], recv.at[src], {"row": src}).wait_recv()
+
+    def to_seats(buf, send, recv):
+        to = [lax.rem(seat + k, SEATS) for k in (4, 5, 3, 6, 2, 7, 1)]
+        start(
+            remote(buf.at[seat], buf.at[seat], send.at[k + 1], recv.at[seat], {"row": device(t, x)})
+            for k, t in enumerate(to)
+        )
+
+    def from_seats(buf, send, recv):
+        for k in range(1, SEATS):
+            src = lax.rem(seat + k, SEATS)
+            remote(buf.at[src], buf.at[src], send.at[k], recv.at[src], {"row": device(src, x)}).wait_recv()
+
+    def tell(part):
         to_list(from_list1.at[part], list1_s.at[part], list1_r.at[part])
 
     def learn(part):
@@ -369,6 +373,7 @@
 
     tell(0)
     row_pass([add(1)])
+    prepare(1)
     tell(1)
 
     learn(0)
@@ -400,6 +405,28 @@
     for b in range(NK // 128):
         from_list3[lst, b : b + 1, :] = jnp.sum(total[b * 128 : (b + 1) * 128, :].T, axis=0, keepdims=True)
     to_list(from_list3, list3_s, list3_r)
+
+    firsts = ((1 - x) * LB, x * LB)
+
+    def seat_at(k):
+        j = lax.div(k, 2)
+        far = j + lax.div(j, 2) - 2 * lax.div(j, 3)
+        return lax.rem(y + far, 4) * 2 + lax.rem(k, 2)
+
+    def late_scores(k, carry):
+        tile = keys_all[seat_at(k)]
+        for side_ in range(2):
+            lists = pl.ds(pl.multiple_of(seat * SHARE + firsts[side_], 128), LB)
+            for h in range(2):
+                s = lax.dot_general(cents[lists, :], tile[h * W : (h + 1) * W], NT_DIMS, preferred_element_type=f32)
+                if side_ == 0:
+                    late[k, h] = s
+                else:
+                    scores[lax.div(k, 2), lax.rem(k, 2), h, 0:LB, :] = s
+        return carry
+
+    gather.arrive((0, 1, 9))
+    lax.fori_loop(0, 6, late_scores, 0)
     from_list(from_list3, list3_s, list3_r)
     delta = -LOG2_KEYS - log2(tree(jnp.add, [from_list3[k] for k in range(N_LIST)]))
     row2 = row1[...] + delta
@@ -410,9 +437,8 @@
     acc[...] = jnp.zeros(acc.shape, f32)
     tsum[...] = jnp.zeros(tsum.shape, f32)
     gather.stage3()
-
-    def base(block):
-        return (block * x + (1 - block) * (1 - x)) * LB
+    gather.arrive((2, 3))
+    lax.fori_loop(6, SEATS, late_scores, 0)
 
     def piece_at(ch):
         def at(y, x, part, of=core):
@@ -432,17 +458,17 @@
     def swap_sums(block):
         return remote(tmine.at[block], tcame.at[block], tsum_s.at[block], tsum_r.at[block], side)
 
-    def sums(block):
-        for b in range(NCH):
+    def sums(side_, pieces):
+        for b in pieces:
             rows = slice(b * 128, (b + 1) * 128)
-            tmine[block, b : b + 1, :] = jnp.sum(tsum[block, rows, :].T, axis=0, keepdims=True)
-        swap_sums(block).start()
+            tmine[side_, b : b + 1, :] = jnp.sum(tsum[side_, rows, :].T, axis=0, keepdims=True)
 
     def hand_over():
+        sums(0, range(NCH))
+        swap_sums(0).start()
         for ch in range(NCH):
             give[ch] = acc[0, ch * PIECE : (ch + 1) * PIECE, :].astype(bf16)
             swap(ch).start()
-        sums(0)
 
     def keep(ch):
         return pltpu.make_async_copy(done.at[ch], piece_at(ch)(y, x, None), here.at[ch])
@@ -460,64 +486,60 @@
 
     def update(block, other):
         for b in range(NCH):
-            at = pl.ds((block * x + (1 - block) * (1 - x)) * NCH + b, 1)
+            at = pl.ds((x if block else 1 - x) * NCH + b, 1)
             whole = tmine[block, b : b + 1, :] + tcame[other, b : b + 1, :]
             pots2[seat, at, :] = pots[seat, at, :] - log2(whole)
 
-    def tile(t):
-        return keys_all[lax.div(t * KT, NK)]
-
-    def mm1(block, t):
-        c = cents[pl.ds(pl.multiple_of(seat * SHARE + base(block), LB), LB), :]
-        return lax.dot_general(c, tile(t), NT_DIMS, preferred_element_type=f32)
-
-    def mm2(w_ref, t):
-        return lax.dot_general(w_ref[...], tile(t), NN_DIMS, preferred_element_type=f32)
-
-    def weigh(s_ref, w_ref, block, t):
-        c = list_lanes[pl.ds(pl.multiple_of(base(block), LB), LB), :]
-        parts = []
-        for v in range(KT // 128):
-            lanes = slice(v * 128, (v + 1) * 128)
-            r = row_lanes[:, pl.ds(pl.multiple_of(t * KT + v * 128, 128), 128)]
-            e = jnp.exp2((s_ref[:, lanes] * SCALE + r) + c)
-            w_ref[:, lanes] = e.astype(bf16)
-            parts.append(e)
-        tsum[block] += tree(jnp.add, parts)
-
-    wb[...] = jnp.zeros(wb.shape, bf16)
+    def run(side_):
+        lists = pl.ds(pl.multiple_of(firsts[side_], 128), LB)
+
+        def sum_up(w_ref, k):
+            return lax.dot_general(w_ref[...], keys_all[seat_at(k)], NN_DIMS, preferred_element_type=f32)
+
+        def weigh(w_ref, k, odd):
+            c = list_lanes[lists, :]
+            parts = []
+            for v in range(NK // 128):
+                h, u = v // (W // 128), v % (W // 128)
+                lanes = slice(u * 128, (u + 1) * 128)
+                s = late[k, h, :, lanes] if side_ == 0 else scores[lax.div(k, 2), odd, h, 0:LB, lanes]
+                r = row_lanes[k, :, v * 128 : (v + 1) * 128]
+                w = jnp.exp2((s * SCALE + r) + c)
+                w_ref[:, v * 128 : (v + 1) * 128] = w.astype(bf16)
+                parts.append(w)
+            tsum[side_] += tree(jnp.add, parts)
+
+        def step(i, carry):
+            before = sum_up(wb, lax.rem(2 * i + SEATS - 1, SEATS))
+            weigh(wa, 2 * i, 0)
+            acc[side_] += before
+            now = sum_up(wa, 2 * i)
+            weigh(wb, 2 * i + 1, 1)
+            acc[side_] += now
+            return carry
+
+        wb[...] = jnp.zeros(wb.shape, bf16)
+        lax.fori_loop(0, SEATS // 2, step, 0)
+        acc[side_] += sum_up(wb, SEATS - 1)
+
     from_seats(row_all, all_s, all_r)
-    gather.arrive()
-    sa[...] = mm1(0, 0)
-    for q in range(SEATS):
+    for k in range(SEATS):
         for b in range(NK // 128):
-            row_lanes[:, (q * 8 + b) * 128 : (q * 8 + b + 1) * 128] = row_all[q, b : b + 1, :]
-
-    def step(i, carry):
-        block, t = lax.div(i, STEPS), 2 * lax.rem(i, STEPS)
-        nxt, prv = lax.rem(i + 1, 2 * STEPS), lax.rem(i + 2 * STEPS - 1, 2 * STEPS)
-        before = mm2(wb, 2 * lax.rem(prv, STEPS) + 1)
-        sb[...] = mm1(block, t + 1)
-        weigh(sa, wa, block, t)
-        acc[lax.div(prv, STEPS)] += before
-        now = mm2(wa, t)
-        sa[...] = mm1(lax.div(nxt, STEPS), 2 * lax.rem(nxt, STEPS))
-        weigh(sb, wb, block, t + 1)
-        acc[block] += now
-        pl.when(i == STEPS)(hand_over)
-        return carry
-
-    lax.fori_loop(0, 2 * STEPS, step, 0)
-    acc[1] += mm2(wb, SEATS * NK // KT - 1)
-    sums(1)
+            row_lanes[k, :, b * 128 : (b + 1) * 128] = row_all[seat_at(k), b : b + 1, :]
+    run(0)
+    hand_over()
+    run(1)
+    sums(1, range(NCH))
     swap_sums(0).wait()
-    for ch in range(NCH):
+    begin(0)
+    swap_sums(1).start()
+    for ch in range(1, NCH):
         begin(ch)
+    outs[0].stage2()
     swap_sums(1).wait()
     update(0, 1)
     update(1, 0)
     to_seats(pots2, pot2_s, pot2_r)
-    outs[0].stage2()
     outs[1].stage2()
     outs[0].stage3()
     outs[2].stage2()
@@ -570,12 +592,11 @@
             pltpu.VMEM((N_ROW, *small), f32),
             pltpu.VMEM((SEATS, *small), f32),
             pltpu.VMEM((SEATS, NK, D), bf16),
-            pltpu.VMEM((1, SEATS * NK), f32),
+            pltpu.VMEM((SEATS, 1, NK), f32),
             pltpu.VMEM((SHARE, 128), f32),
-            pltpu.VMEM((LB, KT), f32),
-            pltpu.VMEM((LB, KT), f32),
-            pltpu.VMEM((LB, KT), bf16),
-            pltpu.VMEM((LB, KT), bf16),
+            pltpu.VMEM((SEATS, 2, LB, W), f32),
+            pltpu.VMEM((LB, NK), bf16),
+            pltpu.VMEM((LB, NK), bf16),
             pltpu.VMEM((2, LB, D), f32),
             pltpu.VMEM((NCH, PIECE, D), bf16),
             pltpu.VMEM((NCH, PIECE, D), bf16),

time: 80.3 us -> 76 us (0.946)
  Pallas kernels: 76.7 us -> 72.3 us
    pallas_call x1, Pallas kernels: 76.7 us -> 72.3 us  [local(): pl.pallas_call(kernel, out_shape=(pltpu.VMEM((NL, D), bf16), jax.ShapeDty...]
where the time goes in v5:
time: 76 us; the launch traced here: 75.9 us
  Pallas kernels  72.3 us (95%)
  local copies, waits for them, and re-layouts  2.88 us (4%)
    pallas_call x1, Pallas kernels, local(): pl.pallas_call(kernel, out_shape=(pltpu.VMEM((NL, D), bf16), jax.ShapeDty...  72.3 us
    unnamed x7, local copies, waits for them, and re-layouts  2.88 us

profile of v5, /device:TPU:1, one launch (start us, length us, event | category | flops | bytes accessed | tf_op | source)
XLA Modules:
  0.0 75.9 jit_solution(5312508877780319311)
XLA Ops:
  0.6 72.3 %sinkhorn.1 = (bf16[6144,256]{1,0:T(8,128)(2,1)S(1)}, f32[8,128]{1,0:T(8,128)}, f32[48,128]{1,0:T(8,128)}) custom-call(bf16[1024,256]{1,0:T(8,128)(2,1)} %keys_hbm.1, bf16[6144,256]{1,0:T(8,128)(2,1)} %cents_hbm.1), custom_call_target="tpu_custom_call" | custom-call | tf_op jit(solution)/shard_map/sinkhorn/pallas_call | solution.py:567
  73.0 0.0 copy-start.1
  73.0 0.0 copy-start
  73.0 1.7 %copy.8 = bf16[6144,256]{1,0:T(8,128)(2,1)} copy(bf16[6144,256]{1,0:T(8,128)(2,1)S(1)} %get-tuple-element.9) | data formatting | bytes 6291456
  74.7 0.0 copy-done.1
  74.7 0.6 copy.9
  75.3 0.0 copy-done
  75.3 0.6 copy.10
Async XLA Ops:
  73.0 1.7 %copy-start.1 = (f32[8,128]{1,0:T(8,128)S(1)}, f32[8,128]{1,0:T(8,128)}, u32[]{:S(2)}) copy-start(f32[8,128]{1,0:T(8,128)} %get-tuple-element.7) | copy-start | bytes 12292
  73.0 2.3 %copy-start = (f32[48,128]{1,0:T(8,128)S(1)}, f32[48,128]{1,0:T(8,128)}, u32[]{:S(2)}) copy-start(f32[48,128]{1,0:T(8,128)} %get-tuple-element.8) | copy-start | bytes 73732

commit v6 on v5

--- a/solution.py
+++ b/solution.py
@@ -159,7 +159,7 @@
 
 
 class Gather:
-    def __init__(self, at, send, recv, y, x, core, own, ring=False):
+    def __init__(self, at, send, recv, y, x, core, own, ring=False, lean=0):
         self.at, self.send, self.recv = at, send, recv
         self.y, self.x, self.core, self.own, self.ring = y, x, core, own, ring
 
@@ -179,6 +179,11 @@
             (side, (-2, False), (2, True), 0),
             (side, (2, False), (2, True), 1),
         ]
+        if lean:
+            m = 5 if lean < 0 else 6
+            block = (-1, False) if lean < 0 else (1, False)
+            self.moves[m] = (side, block, (block[0], True), None)
+        self.lean = lean
         self.used = range(4) if ring else range(9)
 
     def place(self, block, part, *of):
@@ -226,9 +231,9 @@
         self.hand(9).start()
 
     def stage2(self):
-        self.take(0, 2)
-        self.take(1, 3)
-        self.take(4, 5, 6)
+        self.take(0, 2, *((5,) if self.lean < 0 else ()))
+        self.take(1, 3, *((6,) if self.lean > 0 else ()))
+        self.take(4, *((5,) if self.lean >= 0 else ()), *((6,) if self.lean <= 0 else ()))
 
     def stage3(self):
         self.take(2, 7)
@@ -413,16 +418,21 @@
         far = j + lax.div(j, 2) - 2 * lax.div(j, 3)
         return lax.rem(y + far, 4) * 2 + lax.rem(k, 2)
 
+    spread(pots[seat] + LOG2_LISTS, BLOCKS, list_lanes)
+
     def late_scores(k, carry):
         tile = keys_all[seat_at(k)]
         for side_ in range(2):
             lists = pl.ds(pl.multiple_of(seat * SHARE + firsts[side_], 128), LB)
             for h in range(2):
                 s = lax.dot_general(cents[lists, :], tile[h * W : (h + 1) * W], NT_DIMS, preferred_element_type=f32)
-                if side_ == 0:
-                    late[k, h] = s
-                else:
-                    scores[lax.div(k, 2), lax.rem(k, 2), h, 0:LB, :] = s
+                c = list_lanes[pl.ds(pl.multiple_of(firsts[side_], 128), LB), :]
+                for v in range(W // 128):
+                    lanes = slice(v * 128, (v + 1) * 128)
+                    if side_ == 0:
+                        late[k, h, :, lanes] = s[:, lanes] * SCALE + c
+                    else:
+                        scores[lax.div(k, 2), lax.rem(k, 2), h, 0:LB, lanes] = s[:, lanes] * SCALE + c
         return carry
 
     gather.arrive((0, 1, 9))
@@ -433,7 +443,6 @@
     row_all[seat] = row2
     to_seats(row_all, all_s, all_r)
     rowpot_ref[...] = row2 * LN2
-    spread(pots[seat] + LOG2_LISTS, BLOCKS, list_lanes)
     acc[...] = jnp.zeros(acc.shape, f32)
     tsum[...] = jnp.zeros(tsum.shape, f32)
     gather.stage3()
@@ -449,7 +458,10 @@
 
         return at
 
-    outs = [Gather(piece_at(ch), out_s.at[ch], out_r.at[ch], y, x, core, done.at[ch]) for ch in range(NCH)]
+    outs = [
+        Gather(piece_at(ch), out_s.at[ch], out_r.at[ch], y, x, core, done.at[ch], lean=(1, -1, 0)[ch])
+        for ch in range(NCH)
+    ]
     side = {"row": device(seat, 1 - x)}
 
     def swap(ch):
@@ -491,20 +503,17 @@
             pots2[seat, at, :] = pots[seat, at, :] - log2(whole)
 
     def run(side_):
-        lists = pl.ds(pl.multiple_of(firsts[side_], 128), LB)
-
         def sum_up(w_ref, k):
             return lax.dot_general(w_ref[...], keys_all[seat_at(k)], NN_DIMS, preferred_element_type=f32)
 
         def weigh(w_ref, k, odd):
-            c = list_lanes[lists, :]
             parts = []
             for v in range(NK // 128):
                 h, u = v // (W // 128), v % (W // 128)
                 lanes = slice(u * 128, (u + 1) * 128)
                 s = late[k, h, :, lanes] if side_ == 0 else scores[lax.div(k, 2), odd, h, 0:LB, lanes]
                 r = row_lanes[k, :, v * 128 : (v + 1) * 128]
-                w = jnp.exp2((s * SCALE + r) + c)
+                w = jnp.exp2(s + r)
                 w_ref[:, v * 128 : (v + 1) * 128] = w.astype(bf16)
                 parts.append(w)
             tsum[side_] += tree(jnp.add, parts)
@@ -531,18 +540,16 @@
     run(1)
     sums(1, range(NCH))
     swap_sums(0).wait()
-    begin(0)
+    for ch in range(NCH):
+        begin(ch)
     swap_sums(1).start()
-    for ch in range(1, NCH):
-        begin(ch)
-    outs[0].stage2()
+    for ch in range(NCH):
+        outs[ch].stage2()
+    outs[0].stage3()
     swap_sums(1).wait()
     update(0, 1)
     update(1, 0)
     to_seats(pots2, pot2_s, pot2_r)
-    outs[1].stage2()
-    outs[0].stage3()
-    outs[2].stage2()
     outs[1].stage3()
     outs[0].stage4()
     outs[2].stage3()

time: 76 us -> 73.8 us (0.971)
  Pallas kernels: 72.3 us -> 70.1 us
    pallas_call x1, Pallas kernels: 72.3 us -> 70.1 us  [local(): pl.pallas_call(kernel, out_shape=(pltpu.VMEM((NL, D), bf16), jax.ShapeDty...]
where the time goes in v6:
time: 73.8 us; the launch traced here: 73.6 us
  Pallas kernels  70.1 us (95%)
  local copies, waits for them, and re-layouts  2.88 us (4%)
    pallas_call x1, Pallas kernels, local(): pl.pallas_call(kernel, out_shape=(pltpu.VMEM((NL, D), bf16), jax.ShapeDty...  70.1 us
    unnamed x7, local copies, waits for them, and re-layouts  2.88 us

profile of v6, /device:TPU:1, one launch (start us, length us, event | category | flops | bytes accessed | tf_op | source)
XLA Modules:
  0.0 73.6 jit_solution(17335032853602679117)
XLA Ops:
  0.6 70.1 %sinkhorn.1 = (bf16[6144,256]{1,0:T(8,128)(2,1)S(1)}, f32[8,128]{1,0:T(8,128)}, f32[48,128]{1,0:T(8,128)}) custom-call(bf16[1024,256]{1,0:T(8,128)(2,1)} %keys_hbm.1, bf16[6144,256]{1,0:T(8,128)(2,1)} %cents_hbm.1), custom_call_target="tpu_custom_call" | custom-call | tf_op jit(solution)/shard_map/sinkhorn/pallas_call | solution.py:574
  70.7 0.0 copy-start.1
  70.7 0.0 copy-start
  70.8 1.7 %copy.8 = bf16[6144,256]{1,0:T(8,128)(2,1)} copy(bf16[6144,256]{1,0:T(8,128)(2,1)S(1)} %get-tuple-element.9) | data formatting | bytes 6291456
  72.4 0.0 copy-done.1
  72.4 0.6 copy.9
  73.0 0.0 copy-done
  73.0 0.6 copy.10
Async XLA Ops:
  70.7 1.7 %copy-start.1 = (f32[8,128]{1,0:T(8,128)S(1)}, f32[8,128]{1,0:T(8,128)}, u32[]{:S(2)}) copy-start(f32[8,128]{1,0:T(8,128)} %get-tuple-element.7) | copy-start | bytes 12292
  70.7 2.3 %copy-start = (f32[48,128]{1,0:T(8,128)S(1)}, f32[48,128]{1,0:T(8,128)}, u32[]{:S(2)}) copy-start(f32[48,128]{1,0:T(8,128)} %get-tuple-element.8) | copy-start | bytes 73732

commit v7 on v6

--- a/solution.py
+++ b/solution.py
@@ -436,7 +436,7 @@
         return carry
 
     gather.arrive((0, 1, 9))
-    lax.fori_loop(0, 6, late_scores, 0)
+    lax.fori_loop(0, 4, late_scores, 0)
     from_list(from_list3, list3_s, list3_r)
     delta = -LOG2_KEYS - log2(tree(jnp.add, [from_list3[k] for k in range(N_LIST)]))
     row2 = row1[...] + delta
@@ -447,7 +447,7 @@
     tsum[...] = jnp.zeros(tsum.shape, f32)
     gather.stage3()
     gather.arrive((2, 3))
-    lax.fori_loop(6, SEATS, late_scores, 0)
+    lax.fori_loop(4, SEATS, late_scores, 0)
 
     def piece_at(ch):
         def at(y, x, part, of=core):

time: 73.8 us -> 75 us (1.016)
  Pallas kernels: 70.1 us -> 71.3 us
    pallas_call x1, Pallas kernels: 70.1 us -> 71.3 us  [local(): pl.pallas_call(kernel, out_shape=(pltpu.VMEM((NL, D), bf16), jax.ShapeDty...]
where the time goes in v7:
time: 75 us; the launch traced here: 74.9 us
  Pallas kernels  71.3 us (95%)
  local copies, waits for them, and re-layouts  2.88 us (4%)
    pallas_call x1, Pallas kernels, local(): pl.pallas_call(kernel, out_shape=(pltpu.VMEM((NL, D), bf16), jax.ShapeDty...  71.3 us
    unnamed x7, local copies, waits for them, and re-layouts  2.88 us

profile of v7, /device:TPU:1, one launch (start us, length us, event | category | flops | bytes accessed | tf_op | source)
XLA Modules:
  0.0 74.9 jit_solution(6980210149135592500)
XLA Ops:
  0.6 71.3 %sinkhorn.1 = (bf16[6144,256]{1,0:T(8,128)(2,1)S(1)}, f32[8,128]{1,0:T(8,128)}, f32[48,128]{1,0:T(8,128)}) custom-call(bf16[1024,256]{1,0:T(8,128)(2,1)} %keys_hbm.1, bf16[6144,256]{1,0:T(8,128)(2,1)} %cents_hbm.1), custom_call_target="tpu_custom_call" | custom-call | tf_op jit(solution)/shard_map/sinkhorn/pallas_call | solution.py:574
  72.0 0.0 copy-start.1
  72.0 0.0 copy-start
  72.0 1.7 %copy.8 = bf16[6144,256]{1,0:T(8,128)(2,1)} copy(bf16[6144,256]{1,0:T(8,128)(2,1)S(1)} %get-tuple-element.9) | data formatting | bytes 6291456
  73.7 0.0 copy-done.1
  73.7 0.6 copy.9
  74.3 0.0 copy-done
  74.3 0.6 copy.10
Async XLA Ops:
  72.0 1.7 %copy-start.1 = (f32[8,128]{1,0:T(8,128)S(1)}, f32[8,128]{1,0:T(8,128)}, u32[]{:S(2)}) copy-start(f32[8,128]{1,0:T(8,128)} %get-tuple-element.7) | copy-start | bytes 12292
  72.0 2.3 %copy-start = (f32[48,128]{1,0:T(8,128)S(1)}, f32[48,128]{1,0:T(8,128)}, u32[]{:S(2)}) copy-start(f32[48,128]{1,0:T(8,128)} %get-tuple-element.8) | copy-start | bytes 73732
